TPU v7x, 32 devices: a whole 2x2x4 slice. The times are simulated.
32 devices in a mesh: pos: 4 (over x, core), seq: 8 (over z, y).
Axes of the slice: x: 2, y: 2, z: 4, core: 2. Of those that a mesh axis runs over, the one named last changes fastest.
Arguments:
- tokens: bfloat16 [1024, 32, 768], P('pos', 'seq'), may hold values from -6 to 6
- cotangent: bfloat16 [1024, 32, 768], P('pos', 'seq'), may hold values from -6 to 6
- gains: float32 [2, 768], replicated, may hold values from 0.5 to 1.5
- gain_first: float32 [2, 768], replicated, may hold values from -54.3058 to 54.3058
- gain_second: float32 [2, 768], replicated, may hold values from 11.239424 to 80.2816
- mix_logits: float32 [12, 1024, 1024], P(None, None, 'pos'), may hold values from -9 to 9
- logit_first: float32 [12, 1024, 1024], P(None, None, 'pos'), may hold values from -95.57821 to 95.57821, as said below
- logit_second: float32 [12, 1024, 1024], P(None, None, 'pos'), may hold values from 2e-10 to 236.97818, as said below
- w_value: float32 [768, 768], P('seq'), may hold values from -0.21875 to 0.21875
- value_first: float32 [768, 768], P('seq'), may hold values from -63.356766 to 63.356766
- value_second: float32 [768, 768], P('seq'), may hold values from 14.680064 to 104.8576
- w_out: float32 [768, 768], P('seq'), may hold values from -1.75 to 1.75
- out_first: float32 [768, 768], P('seq'), may hold values from -12.44508 to 12.44508
- out_second: float32 [768, 768], P('seq'), may hold values from 0.56 to 4
- w_up: float32 [768, 3072], P('seq'), may hold values from -0.21875 to 0.21875
- up_first: float32 [768, 3072], P('seq'), may hold values from -23.532515 to 23.532515
- up_second: float32 [768, 3072], P('seq'), may hold values from 2.064384 to 14.7456
- w_down: float32 [3072, 768], P('seq'), may hold values from -0.109375 to 0.109375
- down_first: float32 [3072, 768], P('seq'), may hold values from -47.06503 to 47.06503
- down_second: float32 [3072, 768], P('seq'), may hold values from 8.257536 to 58.9824
Outputs:
- output: bfloat16 [1024, 32, 768], P('pos', 'seq')
- input_grad: bfloat16 [1024, 32, 768], P('pos', 'seq')
- gains_new: float32 [2, 768], replicated
- gain_first_new: float32 [2, 768], replicated
- gain_second_new: float32 [2, 768], replicated
- logits_new: float32 [12, 1024, 1024], P(None, None, 'pos')
- logit_first_new: float32 [12, 1024, 1024], P(None, None, 'pos')
- logit_second_new: float32 [12, 1024, 1024], P(None, None, 'pos')
- value_new: float32 [768, 768], P('seq')
- value_first_new: float32 [768, 768], P('seq')
- value_second_new: float32 [768, 768], P('seq')
- out_new: float32 [768, 768], P('seq')
- out_first_new: float32 [768, 768], P('seq')
- out_second_new: float32 [768, 768], P('seq')
- up_new: float32 [768, 3072], P('seq')
- up_first_new: float32 [768, 3072], P('seq')
- up_second_new: float32 [768, 3072], P('seq')
- down_new: float32 [3072, 768], P('seq')
- down_first_new: float32 [3072, 768], P('seq')
- down_second_new: float32 [3072, 768], P('seq')
Inputs may be any that keep to these rules, and one draw needn't show every extreme that they name: `logit_first`: first moments of both signs. `logit_second`: positive.
All inputs are finite; a program needn't handle non-finite values.
Results may differ from a plain program's by a relative error of at most 0.0085.
Values may be sent and summed in bfloat16 or wider, within the bound.
No kernel may reach another device: no remote copies, remote signals or barrier semaphores. Data moves between devices by JAX's collectives and lax.ppermute only.
A program may use at most 256 MiB of HBM per device.

v0:
```python
import math

import jax
import jax.numpy as jnp
from jax import lax
from jax.sharding import PartitionSpec as P

D = 768
FF = 3072
L = 1024
STEP = 10


norm_eps = 1e-05
beta_first = 0.9
beta_second = 0.999
adam_eps = 1e-08
weight_decay = 0.1
hidden_floor = -1e30


def normalize(hidden, gain):
    scale = lax.rsqrt(jnp.mean(hidden * hidden, axis=-1, keepdims=True) + norm_eps)
    return hidden * scale * gain


def gelu_tanh(inputs):
    return jax.nn.gelu(inputs, approximate=True)


def adam_update(weight, first, second, gradient, rate, decay):
    first_new = beta_first * first + (1.0 - beta_first) * gradient
    second_new = beta_second * second + (1.0 - beta_second) * gradient * gradient
    first_hat = first_new / (1.0 - beta_first**STEP)
    second_hat = second_new / (1.0 - beta_second**STEP)
    weight_new = weight - rate * (first_hat / (jnp.sqrt(second_hat) + adam_eps) + decay * weight)
    return (weight_new, first_new, second_new)


def body(
    tokens,
    cotangent,
    gains,
    gain_first,
    gain_second,
    mix_logits,
    logit_first,
    logit_second,
    w_value,
    value_first,
    value_second,
    w_out,
    out_first,
    out_second,
    w_up,
    up_first,
    up_second,
    w_down,
    down_first,
    down_second,
):
    head_count, length, width_pos = mix_logits.shape
    positions, seq_count, width = tokens.shape
    head_size = width // head_count
    token_rows = positions * seq_count
    value_full, out_full, up_full, down_full = (
        lax.all_gather(w_value.astype(jnp.bfloat16), "seq", axis=0, tiled=True),
        lax.all_gather(w_out.astype(jnp.bfloat16), "seq", axis=0, tiled=True),
        lax.all_gather(w_up.astype(jnp.bfloat16), "seq", axis=0, tiled=True),
        lax.all_gather(w_down.astype(jnp.bfloat16), "seq", axis=0, tiled=True),
    )
    row_index = jnp.arange(length, dtype=jnp.int32)
    column_index = lax.axis_index("pos") * width_pos + jnp.arange(width_pos, dtype=jnp.int32)
    visible = (column_index[None, :] <= row_index[:, None])[None]
    masked = jnp.where(visible, mix_logits, hidden_floor)
    local_top = jnp.max(masked, axis=-1)
    row_top = lax.pmax(local_top, "pos")
    local_total = jnp.sum(jnp.where(visible, jnp.exp(masked - row_top[..., None]), 0.0), axis=-1)
    row_total = lax.psum(local_total, "pos")
    attention = jnp.where(visible, jnp.exp(masked - row_top[..., None]), 0.0) / row_total[..., None]
    attention_bf = attention.astype(jnp.bfloat16)
    tokens_wide = tokens.astype(jnp.float32).reshape(token_rows, width)
    normed_in = normalize(tokens_wide, gains[0]).astype(jnp.bfloat16)
    values = jnp.dot(normed_in, value_full, preferred_element_type=jnp.float32).astype(jnp.bfloat16)
    values_heads = values.reshape(positions, seq_count, head_count, head_size)
    mixed_part = jnp.einsum(
        "hij,jshc->ishc", attention_bf, values_heads, preferred_element_type=jnp.float32
    )
    mixed_sum = lax.psum_scatter(
        mixed_part.reshape(positions * lax.axis_size("pos"), seq_count, width),
        "pos",
        scatter_dimension=0,
        tiled=True,
    )
    mixed = mixed_sum.astype(jnp.bfloat16).reshape(token_rows, width)
    hidden = tokens_wide + jnp.dot(mixed, out_full, preferred_element_type=jnp.float32)
    normed_mid = normalize(hidden, gains[1]).astype(jnp.bfloat16)
    up_pre = jnp.dot(normed_mid, up_full, preferred_element_type=jnp.float32)
    active = gelu_tanh(up_pre).astype(jnp.bfloat16)
    output = (hidden + jnp.dot(active, down_full, preferred_element_type=jnp.float32)).astype(
        jnp.bfloat16
    )
    cot_rows = cotangent.reshape(token_rows, width)
    grad_down = jnp.dot(active.T, cot_rows, preferred_element_type=jnp.float32)
    grad_active = jnp.dot(cot_rows, down_full.T, preferred_element_type=jnp.float32)
    gelu_back = jax.vjp(gelu_tanh, up_pre)[1]
    up_grad = gelu_back(grad_active)[0].astype(jnp.bfloat16)
    grad_up = jnp.dot(normed_mid.T, up_grad, preferred_element_type=jnp.float32)
    grad_mid = jnp.dot(up_grad, up_full.T, preferred_element_type=jnp.float32)
    mid_back = jax.vjp(normalize, hidden, gains[1])[1]
    hidden_part, gain_mid = mid_back(grad_mid)
    grad_hidden = cot_rows.astype(jnp.float32) + hidden_part
    hidden_bf = grad_hidden.astype(jnp.bfloat16)
    grad_out = jnp.dot(mixed.T, hidden_bf, preferred_element_type=jnp.float32)
    grad_mixed = jnp.dot(hidden_bf, out_full.T, preferred_element_type=jnp.float32).astype(
        jnp.bfloat16
    )
    mixed_all = lax.all_gather(
        grad_mixed.reshape(positions, seq_count, width), "pos", axis=0, tiled=True
    )
    mixed_heads = mixed_all.reshape(length, seq_count, head_count, head_size)
    grad_scores = jnp.einsum(
        "ishc,jshc->hij", mixed_heads, values_heads, preferred_element_type=jnp.float32
    )
    row_terms = lax.psum(jnp.sum(attention * grad_scores, axis=-1), "pos")
    grad_logits = attention * (grad_scores - row_terms[..., None])
    grad_values = jnp.einsum(
        "hij,ishc->jshc", attention_bf, mixed_heads, preferred_element_type=jnp.float32
    )
    grad_values = grad_values.reshape(token_rows, width).astype(jnp.bfloat16)
    grad_value = jnp.dot(normed_in.T, grad_values, preferred_element_type=jnp.float32)
    grad_in = jnp.dot(grad_values, value_full.T, preferred_element_type=jnp.float32)
    in_back = jax.vjp(normalize, tokens_wide, gains[0])[1]
    token_part, gain_in = in_back(grad_in)
    input_grad = (
        (grad_hidden + token_part).astype(jnp.bfloat16).reshape(positions, seq_count, width)
    )
    logit_total = lax.psum(grad_logits, "seq")
    gain_total = lax.psum(jnp.stack([gain_in, gain_mid]), ("pos", "seq"))
    shards = (
        lax.psum_scatter(grad_value, "seq", scatter_dimension=0, tiled=True),
        lax.psum_scatter(grad_out, "seq", scatter_dimension=0, tiled=True),
        lax.psum_scatter(grad_up, "seq", scatter_dimension=0, tiled=True),
        lax.psum_scatter(grad_down, "seq", scatter_dimension=0, tiled=True),
    )
    totals = lax.psum((shards[0], shards[1], shards[2], shards[3]), "pos")
    gains_new, gain_first_new, gain_second_new = adam_update(
        gains, gain_first, gain_second, gain_total, 0.8, 0.0
    )
    logits_new, logit_first_new, logit_second_new = adam_update(
        mix_logits, logit_first, logit_second, logit_total, 1.5, weight_decay
    )
    value_new, value_first_new, value_second_new = adam_update(
        w_value, value_first, value_second, totals[0], 1.0 / math.sqrt(D), weight_decay
    )
    out_new, out_first_new, out_second_new = adam_update(
        w_out, out_first, out_second, totals[1], 1.0 / math.sqrt(D * 16 // L), weight_decay
    )
    up_new, up_first_new, up_second_new = adam_update(
        w_up, up_first, up_second, totals[2], 1.0 / math.sqrt(D), weight_decay
    )
    down_new, down_first_new, down_second_new = adam_update(
        w_down, down_first, down_second, totals[3], 1.0 / math.sqrt(FF), weight_decay
    )
    return (
        output.reshape(positions, seq_count, width),
        input_grad,
        gains_new,
        gain_first_new,
        gain_second_new,
        logits_new,
        logit_first_new,
        logit_second_new,
        value_new,
        value_first_new,
        value_second_new,
        out_new,
        out_first_new,
        out_second_new,
        up_new,
        up_first_new,
        up_second_new,
        down_new,
        down_first_new,
        down_second_new,
    )


def solution(mesh):
    placed = (
        P("pos", "seq", None),
        P("pos", "seq", None),
        P(),
        P(),
        P(),
        P(None, None, "pos"),
        P(None, None, "pos"),
        P(None, None, "pos"),
        P("seq", None),
        P("seq", None),
        P("seq", None),
        P("seq", None),
        P("seq", None),
        P("seq", None),
        P("seq", None),
        P("seq", None),
        P("seq", None),
        P("seq", None),
        P("seq", None),
        P("seq", None),
    )
    return jax.shard_map(
        body,
        mesh=mesh,
        in_specs=placed,
        out_specs=(
            P("pos", "seq", None),
            P("pos", "seq", None),
            P(),
            P(),
            P(),
            P(None, None, "pos"),
            P(None, None, "pos"),
            P(None, None, "pos"),
            P("seq", None),
            P("seq", None),
            P("seq", None),
            P("seq", None),
            P("seq", None),
            P("seq", None),
            P("seq", None),
            P("seq", None),
            P("seq", None),
            P("seq", None),
            P("seq", None),
            P("seq", None),
        ),
        check_vma=False,
    )
```

profile of v0, /device:TPU:0, one launch (start us, length us, event | category | flops | bytes accessed | tf_op | source)
XLA Modules:
  0.0 1509.6 jit_solution(4638383365321199159)
XLA Ops:
  14.0 12.6 copy.69
  33.1 13.8 pmax.7
  47.0 7.2 fusion.11
  54.2 11.3 psum.56
  73.1 17.7 %fusion.17 = f32[1024,4,12,64]{0,3,1,2:T(8,128)} fusion(bf16[256,4,12,64]{3,2,1,0:T(8,128)(2,1)} %reshape.159, f32[12,1024,256]{1,2,0:T(8,128)} %copy.69, f32[12,1024]{1,0:T(8,128)S(1)} %psum.56, f32[12,1024]{1,0:T(8,128)S(1)} %pmax.7, pred[1024,256]{0,1:T(8,128)(4,1)S(1)} %iota_compare_fusion), kind=kOutput, calls=%fused_computation.29 | convolution fusion | flops 1626341376 | bytes 27099136 | tf_op jit(solution)/shard_map/hij,jshc->ishc/dot_general | solution.py:86
  90.8 12.1 copy.72
  111.9 90.7 %reduce-scatter.6.cloned.1.call-done = f32[256,4,768]{0,2,1:T(8,128)} async-done(((f32[1024,4,768]{0,2,1:T(8,128)}), f32[256,4,768]{0,2,1:T(8,128)}) %reduce-scatter.6.cloned.1.call-update) | async-done | bytes 3145744 | tf_op jit(solution)/shard_map/reduce_scatter | solution.py:89
  209.9 36.5 %all-gather.8.cloned.1.call-done = bf16[768,768]{1,0:T(8,128)(2,1)} async-done(((bf16[96,768]{1,0:T(8,128)(2,1)}), bf16[768,768]{1,0:T(8,128)(2,1)}) %all-gather.8.cloned.1.call-update) | async-done | bytes 1179664 | tf_op jit(solution)/shard_map/all_gather | solution.py:68
  252.1 75.5 %all-gather.10.cloned.1.call-done = bf16[768,3072]{1,0:T(8,128)(2,1)} async-done(((bf16[96,3072]{1,0:T(8,128)(2,1)}), bf16[768,3072]{1,0:T(8,128)(2,1)}) %all-gather.10.cloned.1.call-update) | async-done | bytes 4718608 | tf_op jit(solution)/shard_map/all_gather | solution.py:69
  327.7 11.1 fusion.51
  338.8 69.5 %all-gather.12.cloned.1.call-done = bf16[3072,768]{1,0:T(8,128)(2,1)} async-done(((bf16[384,768]{1,0:T(8,128)(2,1)}), bf16[3072,768]{1,0:T(8,128)(2,1)}) %all-gather.12.cloned.1.call-update) | async-done | bytes 4718608 | tf_op jit(solution)/shard_map/all_gather | solution.py:70
  408.4 14.3 fusion.6
  448.1 36.6 %all-gather.14.cloned.1.call-done = bf16[1024,4,768]{0,2,1:T(8,128)(2,1)} async-done(((bf16[256,4,768]{0,2,1:T(8,128)(2,1)}), bf16[1024,4,768]{0,2,1:T(8,128)(2,1)}) %all-gather.14.cloned.1.call-update) | async-done | bytes 6291472 | tf_op jit(solution)/shard_map/all_gather | solution.py:118
  484.7 10.1 fusion.35
  494.8 6.7 copy.77
  512.6 10.5 fusion.50
  524.6 12.5 fusion.52
  537.1 19.1 %fusion.8 = (f32[12,1024]{1,0:T(8,128)S(1)}, f32[12,1024,256,1]{1,2,0,3:T(8,128)}) fusion(f32[12,1024]{1,0:T(8,128)S(1)} %psum.56, f32[12,1024]{1,0:T(8,128)S(1)} %pmax.7, f32[12,1024,256]{1,2,0:T(8,128)} %copy.69, pred[1024,256]{0,1:T(8,128)(4,1)S(1)} %iota_compare_fusion, bf16[1024,4,12,64]{0,3,2,1:T(8,128)(2,1)} %bitcast.47, ...), kind=kOutput, calls=%fused_computation.13 | convolution fusion | flops 1629474816 | bytes 33439744 | tf_op jit(solution)/shard_map/ishc,jshc->hij/dot_general | solution.py:122
  556.2 11.0 psum.58
  567.2 61.7 %reduce-scatter.8.cloned.1.call-done = f32[96,768]{1,0:T(8,128)} async-done(((f32[768,768]{1,0:T(8,128)}), f32[96,768]{1,0:T(8,128)}) %reduce-scatter.8.cloned.1.call-update) | async-done | bytes 294928 | tf_op jit(solution)/shard_map/reduce_scatter | solution.py:141
  629.0 166.1 %reduce-scatter.12.cloned.1.call-done = f32[96,3072]{1,0:T(8,128)} async-done(((f32[768,3072]{1,0:T(8,128)}), f32[96,3072]{1,0:T(8,128)}) %reduce-scatter.12.cloned.1.call-update) | async-done | bytes 1179664 | tf_op jit(solution)/shard_map/reduce_scatter | solution.py:143
  795.1 166.0 %reduce-scatter.14.cloned.1.call-done = f32[384,768]{1,0:T(8,128)} async-done(((f32[3072,768]{1,0:T(8,128)}), f32[384,768]{1,0:T(8,128)}) %reduce-scatter.14.cloned.1.call-update) | async-done | bytes 1179664 | tf_op jit(solution)/shard_map/reduce_scatter | solution.py:144
  961.2 15.6 %fusion.9 = f32[12,1024,256]{1,2,0:T(8,128)} fusion(f32[12,1024,256,1]{1,2,0,3:T(8,128)} %get-tuple-element.115, f32[12,1024]{1,0:T(8,128)S(1)} %psum.58, f32[12,1024]{1,0:T(8,128)S(1)} %psum.56, f32[12,1024]{1,0:T(8,128)S(1)} %pmax.7, f32[12,1024,256]{1,2,0:T(8,128)} %copy.69, pred[1024,256]{0,1:T(8,128)(4,1)S(1)} %iota_compare_fusion), kind=kLoop, calls=%fused_computation.14 | loop fusion | flops 18874368 | bytes 38158336 | tf_op jit(solution)/shard_map/mul | solution.py:126
  976.8 12.8 copy.78
  989.6 12.8 copy.80
  1002.4 12.9 add_convert_fusion
  1029.1 43.5 %psum.57 = f32[2,768]{1,0:T(2,128)S(1)} all-reduce(f32[2,768]{1,0:T(2,128)S(1)} %pad_maximum_fusion), channel_id=1, replica_groups=mesh['pos'=4,'seq'=8] {'pos','seq'}, use_global_device_ids=true, to_apply=%region_11.12 | all-reduce | flops 1536 | bytes 12288 | tf_op jit(solution)/shard_map/psum | solution.py:139
  1082.5 350.0 %all-reduce.4.cloned.1.call-done = f32[12,1024,256]{1,2,0:T(8,128)} async-done(((f32[12,1024,256]{1,2,0:T(8,128)}), f32[12,1024,256]{1,2,0:T(8,128)}) %all-reduce.4.cloned.1.call-update) | async-done | bytes 12582928 | tf_op jit(solution)/shard_map/psum | solution.py:138
  1432.5 32.1 %multiply_subtract_fusion = (f32[12,1024,256]{1,2,0:T(8,128)}, f32[12,1024,256]{1,2,0:T(8,128)}, f32[12,1024,256]{1,2,0:T(8,128)}) fusion(f32[12,1024,256]{1,2,0:T(8,128)} %copy.69, f32[12,1024,256]{1,2,0:T(8,128)} %all-reduce.4.cloned.1.call-done, f32[12,1024,256]{1,2,0:T(8,128)} %copy.78, f32[12,1024,256]{1,2,0:T(8,128)} %copy.80), kind=kLoop, calls=%fused_computation.15 | loop fusion | flops 47185920 | bytes 88080384 | tf_op jit(solution)/shard_map/sub | solution.py:36
  1464.6 12.6 copy.83
  1477.2 12.6 copy.84
  1489.8 12.6 copy.85
  (139 shorter events, 104.3 us)
Async XLA Ops:
  7.2 4.2 copy-start
  7.2 58.3 %all-gather.6.cloned.1.call-start = ((), (), s32[]{:S(2)}) async-start(), calls=%async_computation.5 | async-start | bytes 1327104 | tf_op jit(solution)/shard_map/all_gather | solution.py:67
  9.0 193.5 %reduce-scatter.6.cloned.1.call-start = ((), (), s32[]{:S(2)}) async-start(), calls=%async_computation.6 | async-start | bytes 15728640 | tf_op jit(solution)/shard_map/reduce_scatter | solution.py:89
  13.9 12.7 copy-start.22
  14.0 51.5 %copy-start.26 = (f32[1024]{0:T(1024)}, f32[1024]{0:T(1024)S(1)}, u32[]{:S(2)}) copy-start(f32[1024]{0:T(1024)S(1)} %rsqrt.25) | copy-start | bytes 12292
  46.9 18.5 %copy-start.24 = (f32[2,768]{1,0:T(2,128)S(1)}, f32[2,768]{1,0:T(2,128)}, u32[]{:S(2)}) copy-start(f32[2,768]{1,0:T(2,128)} %param.22) | copy-start | bytes 18436
  102.9 143.5 %all-gather.8.cloned.1.call-start = ((), (), s32[]{:S(2)}) async-start(), calls=%async_computation.7 | async-start | bytes 1327104 | tf_op jit(solution)/shard_map/all_gather | solution.py:68
  104.5 223.1 %all-gather.10.cloned.1.call-start = ((), (), s32[]{:S(2)}) async-start(), calls=%async_computation.8 | async-start | bytes 5308416 | tf_op jit(solution)/shard_map/all_gather | solution.py:69
  106.8 301.6 %all-gather.12.cloned.1.call-start = ((), (), s32[]{:S(2)}) async-start(), calls=%async_computation.9 | async-start | bytes 5308416 | tf_op jit(solution)/shard_map/all_gather | solution.py:70
  107.7 377.0 %all-gather.14.cloned.1.call-start = ((), (), s32[]{:S(2)}) async-start(), calls=%async_computation.10 | async-start | bytes 7864320 | tf_op jit(solution)/shard_map/all_gather | solution.py:118
  327.7 80.7 %copy-start.4 = (bf16[1024,768]{1,0:T(8,128)(2,1)S(1)}, bf16[1024,768]{1,0:T(8,128)(2,1)}, u32[]{:S(2)}) copy-start(bf16[1024,768]{1,0:T(8,128)(2,1)} %reshape.163) | copy-start | bytes 4718596
  408.4 14.3 copy-start.9
  408.4 14.3 copy-start.31
  422.7 6.0 copy-start.33
  439.2 128.0 %reduce-scatter.10.cloned.1.call-start = ((), (), s32[]{:S(2)}) async-start(), calls=%async_computation.13 | async-start | bytes 2654208 | tf_op jit(solution)/shard_map/reduce_scatter | solution.py:142
  444.5 184.5 %reduce-scatter.8.cloned.1.call-start = ((), (), s32[]{:S(2)}) async-start(), calls=%async_computation.12 | async-start | bytes 2654208 | tf_op jit(solution)/shard_map/reduce_scatter | solution.py:141
  507.6 5.0 copy-start.10
  512.6 282.5 %reduce-scatter.12.cloned.1.call-start = ((), (), s32[]{:S(2)}) async-start(), calls=%async_computation.14 | async-start | bytes 10616832 | tf_op jit(solution)/shard_map/reduce_scatter | solution.py:143
  523.2 437.9 %reduce-scatter.14.cloned.1.call-start = ((), (), s32[]{:S(2)}) async-start(), calls=%async_computation.15 | async-start | bytes 10616832 | tf_op jit(solution)/shard_map/reduce_scatter | solution.py:144
  537.1 536.2 %all-reduce.6.cloned.1.call-start = ((), (), s32[]{:S(2)}) async-start(), calls=%async_computation.16 | async-start | bytes 5898240 | tf_op jit(solution)/shard_map/psum | solution.py:146
  961.2 471.3 %all-reduce.4.cloned.1.call-start = ((), (), s32[]{:S(2)}) async-start(), calls=%async_computation.11 | async-start | bytes 25165824 | tf_op jit(solution)/shard_map/psum | solution.py:138
  989.6 12.8 copy-start.11
  1002.4 17.0 %copy-start.30 = (f32[768]{0:T(1024)S(1)}, f32[768]{0:T(1024)}, u32[]{:S(2)}) copy-start(f32[768]{0:T(1024)} %get-tuple-element.82) | copy-start | bytes 9220
  1015.3 4.0 copy-start.27
  1023.1 50.2 %copy-start.21 = (f32[96,768]{1,0:T(8,128)S(1)}, f32[96,768]{1,0:T(8,128)}, u32[]{:S(2)}) copy-start(f32[96,768]{1,0:T(8,128)} %param.32) | copy-start | bytes 884740
  1025.0 47.6 %copy-start.25 = (f32[2,768]{1,0:T(2,128)S(1)}, f32[2,768]{1,0:T(2,128)}, u32[]{:S(2)}) copy-start(f32[2,768]{1,0:T(2,128)} %param.22) | copy-start | bytes 18436
  1025.0 47.6 %copy-start.28 = (f32[2,768]{1,0:T(2,128)S(1)}, f32[2,768]{1,0:T(2,128)}, u32[]{:S(2)}) copy-start(f32[2,768]{1,0:T(2,128)} %param.23) | copy-start | bytes 18436
  1025.0 47.6 %copy-start.29 = (f32[2,768]{1,0:T(2,128)S(1)}, f32[2,768]{1,0:T(2,128)}, u32[]{:S(2)}) copy-start(f32[2,768]{1,0:T(2,128)} %param.24) | copy-start | bytes 18436
  1025.0 48.2 %copy-start.12 = (f32[96,768]{1,0:T(8,128)S(1)}, f32[96,768]{1,0:T(8,128)}, u32[]{:S(2)}) copy-start(f32[96,768]{1,0:T(8,128)} %param.28) | copy-start | bytes 884740
  1025.0 48.2 %copy-start.14 = (f32[96,768]{1,0:T(8,128)S(1)}, f32[96,768]{1,0:T(8,128)}, u32[]{:S(2)}) copy-start(f32[96,768]{1,0:T(8,128)} %param.31) | copy-start | bytes 884740
  1025.1 51.2 %copy-start.7 = (f32[384,768]{1,0:T(8,128)S(1)}, f32[384,768]{1,0:T(8,128)}, u32[]{:S(2)}) copy-start(f32[384,768]{1,0:T(8,128)} %param.37) | copy-start | bytes 3538948
  1025.1 51.2 %copy-start.15 = (f32[384,768]{1,0:T(8,128)S(1)}, f32[384,768]{1,0:T(8,128)}, u32[]{:S(2)}) copy-start(f32[384,768]{1,0:T(8,128)} %param.38) | copy-start | bytes 3538948
  (14 other events, 39.8 us)
Sparse Core Ops, SparseCore 0:
  10.8 43.7 all-gather.5
  103.0 99.4 reduce-scatter.5
  205.3 41.0 all-gather.7
  249.0 78.6 all-gather.9
  330.3 78.0 all-gather.11
  439.4 45.3 all-gather.13
  488.2 68.9 reduce-scatter.9
  560.7 68.2 reduce-scatter.7
  632.5 162.5 reduce-scatter.11
  798.5 162.5 reduce-scatter.13
  963.7 64.8 all-reduce.5
  1033.8 398.6 all-reduce.3
where the time goes:
time: 1520 us; the launch traced here: 1510 us
  waiting for transfers between devices  1050 us (69%)
  matrix products  140 us (9%)
  local copies, waits for them, and re-layouts  135 us (9%)
  other arithmetic  86 us (6%)
  blocking collectives  79.5 us (5%)
    psum x1, waiting for transfers between devices, body(): logit_total = lax.psum(grad_logits, 'seq')  350 us
    reduce_scatter x1, waiting for transfers between devices, body(): lax.psum_scatter(grad_up, 'seq', scatter_dimension=0, tiled=True)  166 us
    reduce_scatter x1, waiting for transfers between devices, body(): lax.psum_scatter(grad_down, 'seq', scatter_dimension=0, tiled=True)  166 us
    reduce_scatter x1, waiting for transfers between devices, body(): lax.psum_scatter(mixed_part.reshape(positions * lax.axis_size('pos'), seq...  90.7 us
    unnamed x74, local copies, waits for them, and re-layouts  81.5 us
    all_gather x1, waiting for transfers between devices, body(): lax.all_gather(w_up.astype(jnp.bfloat16), 'seq', axis=0, tiled=True)  75.5 us
    all_gather x1, waiting for transfers between devices, body(): lax.all_gather(w_down.astype(jnp.bfloat16), 'seq', axis=0, tiled=True)  69.5 us
    reduce_scatter x1, waiting for transfers between devices, body(): lax.psum_scatter(grad_value, 'seq', scatter_dimension=0, tiled=True)  61.7 us
  transfers between devices with their start and end apart: 12, of which 9 were waited for; matrix products, arithmetic and copies ran while one was open for 14% of the time, Pallas kernels for 0%

commit v1 on v0

v1 whole, which is shorter than its diff:
```python
import functools
import math

import jax
import jax.numpy as jnp
from jax import lax
from jax.experimental import pallas as pl
from jax.experimental.pallas import tpu as pltpu
from jax.sharding import PartitionSpec as P

STEP = 10

norm_eps = 1e-05
beta_first = 0.9
beta_second = 0.999
adam_eps = 1e-08
weight_decay = 0.1
gelu_slope = math.sqrt(2.0 / math.pi)
gelu_cubic = 0.044715

BF = jnp.bfloat16
F32 = jnp.float32
VMEM = 60 * 1024 * 1024
PLAN = "mmuc0mb0i1p1vg2w2wgq3wgwgwg4w5"
LONG, SHORT, FRONT, UPDATE = 200,8,0.5,20
MIX0, MIX1, MIX2 = 200,200,200
GROUP_HEADS = (4, 4, 4)


def bits_of(size):
    return size.bit_length() - 1


def adam_update(weight, first, second, gradient, rate, decay):
    first_new = beta_first * first + (1.0 - beta_first) * gradient
    second_new = beta_second * second + (1.0 - beta_second) * gradient * gradient
    first_hat = first_new / (1.0 - beta_first**STEP)
    second_hat = second_new / (1.0 - beta_second**STEP)
    weight_new = weight - rate * (first_hat / (jnp.sqrt(second_hat) + adam_eps) + decay * weight)
    return (weight_new, first_new, second_new)


def swap(x, axis, mask):
    size = lax.axis_size(axis)
    return lax.ppermute(x, axis, [(i, i ^ mask) for i in range(size)])


def bit_value(axis, bit):
    return (lax.axis_index(axis) >> bit) & 1


def chip_bits(axis):
    return [(axis, b) for b in range(1, bits_of(lax.axis_size(axis)))]


def axis_rank(step):
    axis, bit = step
    return (0 if axis == "seq" else 1, -bit)


def nothing(*refs):
    pass


def behind(x, after, micros=SHORT):
    if not after:
        return x
    anywhere = pl.BlockSpec(memory_space=pl.ANY)
    return pl.pallas_call(
        nothing,
        in_specs=[anywhere] * (1 + len(after)),
        out_specs=anywhere,
        out_shape=jax.ShapeDtypeStruct(x.shape, x.dtype),
        input_output_aliases={0: 0},
        cost_estimate=cost(micros),
        name="behind",
    )(x, *after)


def run(function, *inputs, after=(), micros=SHORT):
    return function(behind(inputs[0], after, micros), *inputs[1:])


class Gather:
    def __init__(self, piece, steps, lead):
        self.out, self.steps, self.lead = piece, list(steps), lead
        self.done = []
        self.shape = (*piece.shape[:lead], -1, piece.shape[-1])
        self.start()

    def start(self):
        if self.steps:
            axis, bit = self.steps[0]
            self.got = swap(self.out, axis, 1 << bit)

    def next(self, after=(), micros=SHORT):
        step = self.steps.pop(0)
        place = self.lead + sum(1 for d in self.done if axis_rank(d) < axis_rank(step))
        high = bit_value(*step) == 1
        self.out = run(
            lambda got, out: jnp.where(
                high, jnp.stack([got, out], axis=place), jnp.stack([out, got], axis=place)
            ),
            self.got,
            self.out,
            after=after,
            micros=micros,
        )
        self.done.append(step)
        self.start()
        return self

    def result(self):
        return self.out.reshape(self.shape)


def bit_array(step):
    return bit_value(*step).astype(jnp.int32).reshape(1)


def halves_kernel(bit_ref, *refs):
    *ins, send_ref, keep_ref = refs
    total = ins[0][...].astype(F32)
    for ref in ins[1:]:
        total = total + ref[...].astype(F32)
    total = total.astype(BF)[:, 0]

    @pl.when(pl.program_id(0) == 0)
    def _():
        send_ref[...] = total

    @pl.when(pl.program_id(0) == 1)
    def _():
        keep_ref[...] = total


def halves_sum(terms, step):
    n, _, rows, columns = terms[0].shape
    blocks = 4 if n % 4 == 0 and n * rows * columns > 1 << 19 else 1
    size = n // blocks
    last = blocks - 1
    return pl.pallas_call(
        halves_kernel,
        grid_spec=pltpu.PrefetchScalarGridSpec(
            num_scalar_prefetch=1,
            grid=(2, blocks),
            in_specs=[
                pl.BlockSpec(
                    (size, 1, rows, columns), lambda i, j, bit: (j, bit[0] ^ (1 - i), 0, 0)
                )
            ]
            * len(terms),
            out_specs=[
                pl.BlockSpec((size, rows, columns), lambda i, j, _: (j * (1 - i) + last * i, 0, 0)),
                pl.BlockSpec((size, rows, columns), lambda i, j, _: (j * i, 0, 0)),
            ],
        ),
        out_shape=[jax.ShapeDtypeStruct((n, rows, columns), BF)] * 2,
        compiler_params=params(),
        cost_estimate=cost(SHORT),
        name="halves_sum",
    )(bit_array(step), *terms)


def sum_kernel(a_ref, b_ref, out_ref):
    out_ref[...] = (a_ref[...].astype(F32) + b_ref[...].astype(F32)).astype(BF)


def sum_of(a, b):
    return pl.pallas_call(
        sum_kernel,
        out_shape=jax.ShapeDtypeStruct(a.shape, BF),
        compiler_params=params(),
        cost_estimate=cost(SHORT),
        name="sum_of",
    )(a, b)


class HalvesOut:
    def __init__(self, send, keep, steps):
        self.steps = list(steps)
        self.columns = send.shape[-1]
        self.send, self.keep = (x.reshape(-1, self.columns) for x in (send, keep))
        self.trade()

    def trade(self):
        axis, bit = self.steps.pop(0)
        self.got = swap(self.send, axis, 1 << bit)

    def next(self, after):
        got = behind(self.got, after)
        terms = [x.reshape(1, 2, -1, self.columns) for x in (self.keep, got)]
        send, keep = halves_sum(terms, self.steps[0])
        self.send, self.keep = send[0], keep[0]
        self.trade()


def pieces_kernel(*refs):
    *ins, out_ref = refs
    for i in range(len(ins) // 2):
        total = ins[2 * i][...].astype(F32) + ins[2 * i + 1][...].astype(F32)
        out_ref[i] = total.astype(BF)


def pieces_of(pairs):
    rows, columns = pairs[0][0].shape
    half = pl.BlockSpec((rows // 2, columns), lambda i: (i, 0))
    return pl.pallas_call(
        pieces_kernel,
        grid=(2,),
        in_specs=[half] * (2 * len(pairs)),
        out_specs=pl.BlockSpec((len(pairs), rows // 2, columns), lambda i: (0, i, 0)),
        out_shape=jax.ShapeDtypeStruct((len(pairs), rows, columns), BF),
        compiler_params=params(),
        cost_estimate=cost(SHORT),
        name="pieces",
    )(*[x for pair in pairs for x in pair])


class RowSum:
    def __init__(self, keep, got, lead, steps, dims):
        self.keep, self.got, self.lead = keep, got, lead
        self.steps, self.left = list(steps), list(dims)
        self.columns = keep.shape[-1]

    def next(self, after):
        step = self.steps.pop(0)
        place = self.left.index(step)
        shape = (self.lead << place, 2, -1, self.columns)
        got = behind(self.got, after)
        send, self.keep = halves_sum([t.reshape(shape) for t in (self.keep, got)], step)
        axis, bit = step
        self.got = swap(send, axis, 1 << bit)
        self.left.remove(step)
        return send


def send_to_queries(blocks):
    size = lax.axis_size("pos")
    blocks = dict(enumerate(blocks))
    own = [blocks[0]]
    sent = None
    for bit in range(bits_of(size)):
        mask = 1 << bit
        for r in sorted((k for k in blocks if k & mask), reverse=True):
            pairs = [(p, p ^ mask) for p in range(size) if (p & ~(mask - 1)) <= (p ^ r)]
            sent = blocks.pop(r)
            got = lax.ppermute(sent, "pos", pairs)
            if r == mask:
                own.append(got)
            else:
                blocks[r ^ mask] = (blocks[r ^ mask].astype(F32) + got.astype(F32)).astype(BF)
    return own, sent


def gather_queries(own, bits, blocks=None):
    size = lax.axis_size("pos")
    blocks = dict(blocks or {0: own})
    for bit in bits:
        mask = 1 << bit
        for r in sorted(blocks):
            if r | mask in blocks:
                continue
            pairs = [
                (p ^ mask, p) for p in range(size) if (p & ~(mask - 1)) <= (p ^ r ^ mask)
            ]
            blocks[r | mask] = lax.ppermute(blocks[r], "pos", pairs)
    return blocks


def params():
    return pltpu.CompilerParams(vmem_limit_bytes=VMEM)


def cost(micros):
    return pl.CostEstimate(flops=int(micros * 1e9), bytes_accessed=0, transcendentals=0)


def column_of(table, index):
    lane = lax.broadcasted_iota(jnp.int32, table.shape, 1)
    return jnp.sum(jnp.where(lane == index, table, 0.0), axis=1, keepdims=True)


def lower(rows, columns):
    return lax.broadcasted_iota(jnp.int32, (rows, columns), 1) <= lax.broadcasted_iota(
        jnp.int32, (rows, columns), 0
    )


def dot(left, right, contract):
    return lax.dot_general(left, right, (contract, ((), ())), preferred_element_type=F32)


def totals_kernel(blocks, pos_ref, logits_ref, *refs):
    out_ref, acc_ref = refs[-2:]
    pair = pl.program_id(0)
    heads, length, width = logits_ref.shape
    me = pos_ref[0]

    @pl.when(pair == 0)
    def _():
        acc_ref[...] = jnp.zeros_like(acc_ref)

    lane = lax.broadcasted_iota(jnp.int32, (width, acc_ref.shape[1]), 1)
    for q in range(blocks):

        @pl.when(q >= me)
        def _(q=q):
            rows = pl.ds(q * width, width)
            acc = acc_ref[rows, :]
            for h in range(heads):
                e = jnp.exp(logits_ref[h, rows, :])
                e = jnp.where(lower(width, width) | (q > me), e, 0.0)
                acc = jnp.where(lane == pair * heads + h, jnp.sum(e, axis=1, keepdims=True), acc)
            acc_ref[rows, :] = acc

    @pl.when(pair == pl.num_programs(0) - 1)
    def _():
        out_ref[...] = acc_ref[...].T[:16]


def row_totals(pos, logits, blocks, after):
    heads, length, width = logits.shape
    return pl.pallas_call(
        functools.partial(totals_kernel, blocks),
        grid_spec=pltpu.PrefetchScalarGridSpec(
            num_scalar_prefetch=1,
            grid=(heads // 2,),
            in_specs=[pl.BlockSpec((2, length, width), lambda m, _: (m, 0, 0))]
            + [pl.BlockSpec(memory_space=pl.ANY)] * len(after),
            out_specs=pl.BlockSpec((16, length), lambda m, _: (0, 0)),
            scratch_shapes=[pltpu.VMEM((length, 128), F32)],
        ),
        out_shape=jax.ShapeDtypeStruct((16, length), F32),
        compiler_params=params(),
        cost_estimate=cost(FRONT),
        name="row_totals",
    )(pos, logits, *after)


def attention_kernel(blocks, pos_ref, logits_ref, scale_ref, out_ref):
    pair = pl.program_id(0)
    heads, length, width = logits_ref.shape
    me = pos_ref[0]
    for q in range(blocks):
        rows = pl.ds(q * width, width)

        @pl.when(q >= me)
        def _(rows=rows, q=q):
            scale = scale_ref[:, rows].T
            for h in range(heads):
                a = jnp.exp(logits_ref[h, rows, :]) * column_of(scale, pair * heads + h)
                a = jnp.where(lower(width, width) | (q > me), a, 0.0)
                out_ref[h, rows, :] = a.astype(BF)

        @pl.when(q < me)
        def _(rows=rows):
            for h in range(heads):
                out_ref[h, rows, :] = jnp.zeros((width, width), BF)


def attention_of(pos, logits, scale, blocks):
    heads, length, width = logits.shape
    pair = pl.BlockSpec((2, length, width), lambda m, _: (m, 0, 0))
    return pl.pallas_call(
        functools.partial(attention_kernel, blocks),
        grid_spec=pltpu.PrefetchScalarGridSpec(
            num_scalar_prefetch=1,
            grid=(heads // 2,),
            in_specs=[pair, pl.BlockSpec((16, length), lambda m, _: (0, 0))],
            out_specs=pair,
        ),
        out_shape=jax.ShapeDtypeStruct(logits.shape, BF),
        compiler_params=params(),
        cost_estimate=cost(FRONT),
        name="attention",
    )(pos, logits, scale)


def half_mask(rows, columns, half):
    lane = lax.broadcasted_iota(jnp.int32, (rows, columns), 1)
    return ((lane >> 6) & 1) == half


def split_heads(wide):
    zero = jnp.zeros_like(wide)
    first = half_mask(wide.shape[0], wide.shape[1], 0)
    return jnp.concatenate([jnp.where(first, wide, zero), jnp.where(first, zero, wide)], axis=0)


def forward_kernel(blocks, pos_ref, attention_ref, values_ref, *outs):
    *outs, all_ref = outs
    width = attention_ref.shape[2]
    seqs = values_ref.shape[0]
    me = pos_ref[0]
    values = split_heads(jnp.concatenate([values_ref[s] for s in range(seqs)], axis=1))
    both = jnp.concatenate([attention_ref[0], attention_ref[1]], axis=1)
    all_ref[...] = dot(both, values, ((1,), (0,))).astype(BF)
    for r in range(blocks):
        rows = pl.ds(pl.multiple_of((me ^ r) * width, width), width)
        for s in range(seqs):
            outs[r][s] = all_ref[rows, s * 128 : s * 128 + 128]


def mix_forward(pos, attention, values, blocks):
    heads, length, width = attention.shape
    seqs, _, wide = values.shape
    part = pl.BlockSpec((seqs, width, 128), lambda m, _: (0, 0, m))
    return pl.pallas_call(
        functools.partial(forward_kernel, blocks),
        grid_spec=pltpu.PrefetchScalarGridSpec(
            num_scalar_prefetch=1,
            grid=(heads // 2,),
            in_specs=[pl.BlockSpec((2, length, width), lambda m, _: (m, 0, 0)), part],
            out_specs=[part] * blocks,
            scratch_shapes=[pltpu.VMEM((length, seqs * 128), BF)],
        ),
        out_shape=[jax.ShapeDtypeStruct((seqs, width, wide), BF)] * blocks,
        compiler_params=params(),
        cost_estimate=cost(FRONT),
        name="mix_forward",
    )(pos, attention, values)


def ffn_kernel(parts, core_ref, *refs):
    (own_ref, got_ref, tokens_ref, cot_ref, gain_ref), refs = refs[:5], refs[5:]
    part_refs, refs = refs[:parts], refs[parts:]
    (
        output_ref,
        mixed_ref,
        normed_ref,
        active_ref,
        up_grad_ref,
        grad_hidden_ref,
        hidden_bf_ref,
        *group_refs,
        gain_grad_ref,
        wa,
        wb,
        product,
        sems,
    ) = refs
    step = pl.program_id(0)
    core = core_ref[0]
    half = own_ref.shape[-1]
    rows, width = tokens_ref.shape[1:]
    mine = pl.ds(pl.multiple_of(core * half, half), half)
    theirs = pl.ds(pl.multiple_of((1 - core) * half, half), half)

    @pl.when(step == 0)
    def _():
        copies = []
        for ref, lanes, sem in ((own_ref, mine, 0), (got_ref, theirs, 1)):
            for u in range(wa.shape[0]):
                copies.append((ref.at[:, u], wa.at[u, :, :, :, lanes], sems.at[sem, u]))
            for j in range(wb.shape[2]):
                u = wa.shape[0] + j
                copies.append((ref.at[:, u], wb.at[:, :, j, :, lanes], sems.at[sem, u]))
        copies = [pltpu.make_async_copy(*copy) for copy in copies]
        for copy in copies:
            copy.start()
        for copy in copies:
            copy.wait()
        product[...] = jnp.zeros_like(product)
        gain_grad_ref[...] = jnp.zeros_like(gain_grad_ref)
        for ref in group_refs:
            ref[...] = jnp.zeros_like(ref)

    w_out = wa[0].reshape(width, width)
    gain = gain_ref[...]
    mixed = part_refs[0][0].astype(F32)
    for ref in part_refs[1:]:
        mixed = mixed + ref[0].astype(F32)
    mixed = mixed.astype(BF)
    mixed_ref[0] = mixed
    hidden = tokens_ref[0].astype(F32) + dot(mixed, w_out, ((1,), (0,)))
    scale = lax.rsqrt(jnp.mean(hidden * hidden, axis=1, keepdims=True) + norm_eps)
    normed = (hidden * scale * gain).astype(BF)
    normed_ref[0] = normed
    cot = cot_ref[0]
    out = hidden
    grad_mid = jnp.zeros((rows, width), F32)
    for j in range(active_ref.shape[0]):
        if wb.shape[0] == 1:
            down = wb[0, 0, j]
        else:
            owners = wb.shape[0] // active_ref.shape[0]
            down = wb[j * owners : (j + 1) * owners].reshape(width, width)
        up = wa[1 + j].reshape(width, width)
        u = dot(normed, up, ((1,), (0,)))
        ga = dot(cot, down, ((1,), (1,)))
        square = u * u
        t = jnp.tanh(u * (gelu_slope + gelu_slope * gelu_cubic * square))
        plus = 0.5 + 0.5 * t
        active = (u * plus).astype(BF)
        slope = plus + (0.5 * u) * (1.0 - t * t) * (
            gelu_slope + 3.0 * gelu_slope * gelu_cubic * square
        )
        up_grad = (ga * slope).astype(BF)
        active_ref[j, 0] = active
        up_grad_ref[j, 0] = up_grad
        out = out + dot(active, down, ((1,), (0,)))
        grad_mid = grad_mid + dot(up_grad, up, ((1,), (1,)))
    output_ref[0] = out.astype(BF)
    gain_grad_ref[...] += jnp.sum(grad_mid * hidden * scale, axis=0, keepdims=True)
    weighted = grad_mid * gain
    inner = jnp.mean(weighted * hidden, axis=1, keepdims=True)
    grad_hidden = cot.astype(F32) + scale * weighted - hidden * (scale * scale * scale * inner)
    grad_hidden_ref[0] = grad_hidden
    hidden_bf = grad_hidden.astype(BF)
    hidden_bf_ref[0] = hidden_bf
    grad_mixed = dot(hidden_bf, w_out, ((1,), (1,))).astype(BF)
    place = pl.ds(pl.multiple_of(step * rows, rows), rows)
    cuts = []
    for ref in group_refs:
        first = cuts[-1].stop if cuts else 0
        cuts.append(slice(first, first + ref.shape[2]))
        ref[0, place, :] = grad_mixed[:, cuts[-1]]
    product[...] += grad_mixed.astype(F32) * mixed.astype(F32)

    @pl.when(step == pl.num_programs(0) - 1)
    def _():
        for ref, cut in zip(group_refs, cuts):
            lanes = cut.stop - cut.start
            head = lax.broadcasted_iota(jnp.int32, (8, lanes), 0)
            lane = lax.broadcasted_iota(jnp.int32, (8, lanes), 1)
            terms = lax.dot_general(
                jnp.where((lane >> 6) == head, 1.0, 0.0),
                product[:, cut],
                (((1,), (1,)), ((), ())),
                precision=lax.Precision.HIGHEST,
                preferred_element_type=F32,
            )
            ref[0, ref.shape[1] - 16 :, :rows] = two_parts(terms)


def two_parts(x):
    high = x.astype(BF).astype(F32)
    return jnp.concatenate([high, x - high], axis=0).astype(BF)


def one_part(x):
    count = x.shape[0] // 2
    x = x.astype(F32)
    return x[:count] + x[count:]


def feed_forward(core, own, got, tokens, cot, gain, parts, group_heads):
    seqs, rows, width = tokens.shape
    n_seq, units, chips, part_rows, _ = own.shape
    count = (units - 1) // 2
    act = pl.BlockSpec((1, rows, width), lambda s, _: (s, 0, 0))
    wide = pl.BlockSpec((count, 1, rows, width), lambda s, _: (0, s, 0, 0))
    payloads = [(1, seqs * rows + 16, 64 * heads) for heads in group_heads]
    anywhere = pl.BlockSpec(memory_space=pl.ANY)
    gain_spec = pl.BlockSpec((1, width), lambda s, _: (0, 0))
    act_bf = jax.ShapeDtypeStruct(tokens.shape, BF)
    wide_bf = jax.ShapeDtypeStruct((count, *tokens.shape), BF)
    tokens_all = seqs * rows
    return pl.pallas_call(
        functools.partial(ffn_kernel, len(parts)),
        grid_spec=pltpu.PrefetchScalarGridSpec(
            num_scalar_prefetch=1,
            grid=(seqs,),
            in_specs=[anywhere] * 2 + [act, act, gain_spec] + [act] * len(parts),
            out_specs=[act, act, act, wide, wide, act, act]
            + [pl.BlockSpec(payload, lambda s, _: (0, 0, 0)) for payload in payloads]
            + [gain_spec],
            scratch_shapes=[
                pltpu.VMEM((1 + count, n_seq, chips, part_rows, width), BF),
                pltpu.VMEM((n_seq, chips, count, part_rows, width), BF),
                pltpu.VMEM((rows, width), F32),
                pltpu.SemaphoreType.DMA((2, units)),
            ],
        ),
        out_shape=[act_bf] * 3
        + [wide_bf] * 2
        + [jax.ShapeDtypeStruct(tokens.shape, F32), act_bf]
        + [jax.ShapeDtypeStruct(payload, BF) for payload in payloads]
        + [jax.ShapeDtypeStruct((1, width), F32)],
        compiler_params=params(),
        cost_estimate=cost(SHORT),
        name="feed_forward",
    )(core, own, got, tokens, cot, gain, *parts)


def write_halves(core, grad, keep_ref, send_ref):
    half = keep_ref.shape[-1]
    for c in range(2):

        @pl.when(core == c)
        def _(c=c):
            keep_ref[0] = grad[:, c * half : c * half + half]
            send_ref[0] = grad[:, half - c * half : 2 * half - c * half]


def grads_kernel(first, core_ref, *refs):
    keep_ref, send_ref = refs[-2:]
    ins = refs[: 4 if first else 2]

    def write(left, right):
        grad = dot(
            left[...].reshape(left.shape[-2:]), right[...].reshape(right.shape[-2:]), ((0,), (0,))
        )
        write_halves(core_ref[0], grad.astype(BF), keep_ref, send_ref)

    if first:
        pl.when(pl.program_id(0) == 0)(lambda: write(ins[0], ins[1]))
        pl.when(pl.program_id(0) > 0)(lambda: write(ins[2], ins[3]))
    else:
        write(*ins)


def weight_grads(core, name, one, many, into=()):
    first = 1 if one else 0
    units = first + max(a.shape[0] for a in many if a.ndim == 3)
    rows, width = many[0].shape[-2:]

    def spec(a):
        if a.ndim == 2:
            return pl.BlockSpec((rows, width), lambda u, _: (0, 0))
        return pl.BlockSpec((1, rows, width), lambda u, _: (jnp.maximum(u - first, 0), 0, 0))

    ins = [*one, *many]
    out = pl.BlockSpec((1, width, width // 2), lambda u, _: (u, 0, 0))
    total = into[0].shape[0] if into else units
    return pl.pallas_call(
        functools.partial(grads_kernel, first),
        grid_spec=pltpu.PrefetchScalarGridSpec(
            num_scalar_prefetch=1,
            grid=(units,),
            in_specs=[spec(a) for a in ins] + [pl.BlockSpec(memory_space=pl.ANY)] * len(into),
            out_specs=[out, out],
        ),
        out_shape=[jax.ShapeDtypeStruct((total, width, width // 2), BF)] * 2,
        input_output_aliases={1 + len(ins) + i: i for i in range(len(into))},
        compiler_params=params(),
        cost_estimate=cost(SHORT),
        name=name,
    )(core, *ins, *into)


def pair_of(step, place_ref, split):
    return (1 - step) ^ place_ref[1] if split else step


def backward_kernel(blocks, split, place_ref, attention_ref, values_ref, *refs):
    grads, terms, refs = refs[:blocks], refs[blocks : 2 * blocks], refs[2 * blocks :]
    *outs, grad_values_ref, acc_ref, all_ref = refs
    step = pl.program_id(0)
    pair = pair_of(step, place_ref, split)
    _, length, width = attention_ref.shape
    seqs = values_ref.shape[0]
    me = place_ref[0]
    values = split_heads(jnp.concatenate([values_ref[s] for s in range(seqs)], axis=1))
    lane = lax.broadcasted_iota(jnp.int32, (width, 8), 1)

    for r in range(blocks):
        q = me ^ r

        @pl.when(q >= me)
        def _(r=r, q=q):
            rows = pl.ds(pl.multiple_of(q * width, width), width)
            grad = jnp.concatenate(
                [grads[r][0, s * width : (s + 1) * width, :] for s in range(seqs)], axis=1
            )
            scores = dot(grad, values, ((1,), (1,)))
            table = one_part(terms[r][0][:, :width]).T
            for h in range(2):
                term = jnp.sum(jnp.where(lane == pair * 2 + h, table, 0.0), axis=1, keepdims=True)
                a = attention_ref[h, rows, :].astype(F32)
                grad_a = (a * (scores[:, h * width : (h + 1) * width] - term)).astype(BF)
                all_ref[h, r] = grad_a
            part = dot(
                jnp.concatenate([attention_ref[0, rows, :], attention_ref[1, rows, :]], axis=0),
                split_heads(grad),
                ((0,), (0,)),
            )
            if r == 0:
                acc_ref[...] = part
            else:
                acc_ref[...] += part

        if r:

            @pl.when(q < me)
            def _(r=r):
                for h in range(2):
                    all_ref[h, r] = jnp.zeros((width, width), BF)

    if split:
        for i, out in enumerate(outs):

            @pl.when(step == i)
            def _(out=out):
                out[...] = all_ref[...]

    else:
        outs[0][...] = all_ref[...]

    total = acc_ref[...].astype(BF)
    for s in range(seqs):
        grad_values_ref[s] = total[:, s * 128 : s * 128 + 128]


def mix_backward(place, attention, values, grads, first, split):
    blocks = len(grads)
    _, length, width = attention.shape
    seqs = values.shape[0]
    lanes = grads[0].shape[2]
    pairs = lanes // 128
    before = first // 2

    def pair(m, at):
        return pair_of(m, at, split)

    part = pl.BlockSpec((1, seqs * width, 128), lambda m, at: (0, 0, pair(m, at)))
    terms = pl.BlockSpec((1, 16, lanes), lambda m, _: (0, seqs * width // 16, 0))
    out = pl.BlockSpec((2, blocks, width, width), lambda m, _: (0 if split else m, 0, 0, 0))
    outs = 2 if split else 1
    rows = 2 if split else 2 * pairs
    return pl.pallas_call(
        functools.partial(backward_kernel, blocks, split),
        grid_spec=pltpu.PrefetchScalarGridSpec(
            num_scalar_prefetch=1,
            grid=(pairs,),
            in_specs=[
                pl.BlockSpec((2, length, width), lambda m, at: (pair(m, at) + before, 0, 0)),
                pl.BlockSpec((seqs, width, 128), lambda m, at: (0, 0, pair(m, at) + before)),
            ]
            + [part] * blocks
            + [terms] * blocks,
            out_specs=[out] * outs
            + [pl.BlockSpec((seqs, width, 128), lambda m, at: (0, 0, pair(m, at)))],
            scratch_shapes=[
                pltpu.VMEM((width, seqs * 128), F32),
                pltpu.VMEM((2, blocks, width, width), BF),
            ],
        ),
        out_shape=[jax.ShapeDtypeStruct((rows, blocks, width, width), BF)] * outs
        + [jax.ShapeDtypeStruct((seqs, width, lanes), BF)],
        compiler_params=params(),
        cost_estimate=cost((MIX0, MIX1, MIX2)[first // 4 % 3]),
        name="mix_backward",
    )(place, attention, values, *grads, *grads)


def logits_adam_kernel(place_ref, weight_ref, first_ref, second_ref, *refs):
    grads, outs = refs[:4], refs[-3:]
    q = pl.program_id(1)
    me = place_ref[0]

    def update(h, gradient):
        weight = weight_ref[h]
        first = beta_first * first_ref[h]
        second = beta_second * second_ref[h]
        if gradient is not None:
            first = first + (1.0 - beta_first) * gradient
            second = second + ((1.0 - beta_second) * gradient) * gradient
        root = second * lax.rsqrt(second)
        bottom = root * math.sqrt(1.0 / (1.0 - beta_second**STEP)) + adam_eps
        step = first * (1.5 / (1.0 - beta_first**STEP)) / bottom
        outs[0][h] = weight * (1.0 - 1.5 * weight_decay) - step
        outs[1][h] = first
        outs[2][h] = second

    @pl.when(q >= me)
    def _():
        for h in range(4):
            update(h, grads[h][0, 0, 0].astype(F32))

    @pl.when(q < me)
    def _():
        for h in range(4):
            update(h, None)


def logits_adam(place, logits, first, second, pieces, group, start, before):
    heads, length, width = logits.shape
    blocks = length // width
    n_seq, groups, rows, _ = pieces.shape
    per = rows // width
    part = pl.BlockSpec((4, width, width), lambda k, q, _: (k + start // 4, q, 0))

    def owner(h, r):
        out = (h >> 1) + 2 * (h & 1)
        left, bit = blocks // 2, 4
        while left >= per:
            out = out + bit * ((r // left) % 2)
            left, bit = left // 2, bit * 2
        return out

    def grad(h):
        def index(k, q, at):
            r = jnp.where(q >= at[0], q ^ at[0], 0)
            return (owner(h, r), k + group, r % per, 0, 0)

        return pl.BlockSpec((1, 1, 1, width, width), index)

    ins = [logits, first, second] + [pieces.reshape(n_seq, groups, per, width, width)] * 4
    specs = [part] * 3 + [grad(h) for h in range(4)]
    aliases = {}
    if before is not None:
        aliases = {1 + len(ins) + i: i for i in range(3)}
        ins += list(before)
        specs += [pl.BlockSpec(memory_space=pl.ANY)] * 3
    return pl.pallas_call(
        logits_adam_kernel,
        grid_spec=pltpu.PrefetchScalarGridSpec(
            num_scalar_prefetch=1,
            grid=(1, blocks),
            in_specs=specs,
            out_specs=[part] * 3,
        ),
        out_shape=[jax.ShapeDtypeStruct(logits.shape, F32)] * 3,
        input_output_aliases=aliases,
        compiler_params=params(),
        cost_estimate=cost(UPDATE),
        name="logits_adam",
    )(place, *ins)


def input_kernel(groups, core_ref, *refs):
    grads, refs = refs[:groups], refs[groups:]
    (normed_ref, tokens_ref, value_ref, hidden_ref, gain_ref), refs = refs[:5], refs[5:]
    input_grad_ref, gain_grad_ref, keep_ref, send_ref, acc_ref = refs
    step = pl.program_id(0)
    grad = jnp.concatenate([ref[0] for ref in grads], axis=1)
    product = dot(normed_ref[0], grad, ((0,), (0,)))
    gain = gain_ref[...]
    tokens = tokens_ref[0].astype(F32)
    scale = lax.rsqrt(jnp.mean(tokens * tokens, axis=1, keepdims=True) + norm_eps)
    grad_in = dot(grad, value_ref[...], ((1,), (1,)))
    gain_part = jnp.sum(grad_in * tokens * scale, axis=0, keepdims=True)
    weighted = grad_in * gain
    inner = jnp.mean(weighted * tokens, axis=1, keepdims=True)
    total = hidden_ref[0] + scale * weighted - tokens * (scale * scale * scale * inner)
    input_grad_ref[0] = total.astype(BF)

    @pl.when(step == 0)
    def _():
        acc_ref[...] = product
        gain_grad_ref[...] = gain_part

    @pl.when(step > 0)
    def _():
        acc_ref[...] += product
        gain_grad_ref[...] += gain_part

    @pl.when(step == pl.num_programs(0) - 1)
    def _():
        write_halves(core_ref[0], acc_ref[...].astype(BF), keep_ref, send_ref)


def input_backward(core, grads, normed, tokens, value, hidden, gain):
    seqs, rows, width = tokens.shape
    act = pl.BlockSpec((1, rows, width), lambda s, _: (s, 0, 0))
    gain_spec = pl.BlockSpec((1, width), lambda s, _: (0, 0))
    half = pl.BlockSpec((1, width, width // 2), lambda s, _: (0, 0, 0))
    return pl.pallas_call(
        functools.partial(input_kernel, len(grads)),
        grid_spec=pltpu.PrefetchScalarGridSpec(
            num_scalar_prefetch=1,
            grid=(seqs,),
            in_specs=[
                pl.BlockSpec((1, rows, grad.shape[2]), lambda s, _: (s, 0, 0)) for grad in grads
            ]
            + [act, act, pl.BlockSpec((width, width), lambda s, _: (0, 0)), act, gain_spec],
            out_specs=[act, gain_spec, half, half],
            scratch_shapes=[pltpu.VMEM((width, width), F32)],
        ),
        out_shape=[
            jax.ShapeDtypeStruct(tokens.shape, BF),
            jax.ShapeDtypeStruct((1, width), F32),
            jax.ShapeDtypeStruct((1, width, width // 2), BF),
            jax.ShapeDtypeStruct((1, width, width // 2), BF),
        ],
        compiler_params=params(),
        cost_estimate=cost(SHORT),
        name="input_backward",
    )(core, *grads, normed, tokens, value, hidden, gain)


def bundle_kernel(keep_a, got_a, keep_b, got_b, out_ref):
    a = keep_a[...].astype(F32) + got_a[...].astype(F32)
    b = keep_b[...].astype(F32) + got_b[...].astype(F32)
    units = a.shape[0]
    out_ref[0, :units] = a[:, 0].astype(BF)
    out_ref[0, units:] = b[0].astype(BF)


def bundle(keep_a, got_a, keep_b, got_b):
    units, owners, rows, columns = keep_a.shape
    units_b = keep_b.shape[1]
    spec_a = pl.BlockSpec((units, 1, rows, columns), lambda g: (0, g, 0, 0))
    spec_b = pl.BlockSpec((1, units_b, rows, columns), lambda g: (g, 0, 0, 0))
    return pl.pallas_call(
        bundle_kernel,
        grid=(owners,),
        in_specs=[spec_a, spec_a, spec_b, spec_b],
        out_specs=pl.BlockSpec((1, units + units_b, rows, columns), lambda g: (g, 0, 0, 0)),
        out_shape=jax.ShapeDtypeStruct((owners, units + units_b, rows, columns), BF),
        compiler_params=params(),
        cost_estimate=cost(SHORT),
        name="bundle",
    )(keep_a, got_a, keep_b, got_b)


def merge_kernel(bit_ref, keep, got, value_keep, value_got, send_ref, keep_ref):
    value = (value_keep[:, 0].astype(F32) + value_got[:, 0].astype(F32)).astype(BF)
    others = (keep[:, 0].astype(F32) + got[:, 0].astype(F32)).astype(BF)
    for i, out in enumerate((send_ref, keep_ref)):

        @pl.when(pl.program_id(0) == i)
        def _(out=out):
            out[:, : others.shape[1]] = others
            out[:, others.shape[1] :] = value


def merge_halves(terms, step):
    n, _, units, rows, columns = terms[0].shape
    total = units + terms[2].shape[2]

    def spec(count):
        return pl.BlockSpec(
            (size, 1, count, rows, columns), lambda i, g, bit: (g, bit[0] ^ (1 - i), 0, 0, 0)
        )

    size = max(1, n // 4)
    last = n // size - 1
    block = (size, total, rows, columns)
    return pl.pallas_call(
        merge_kernel,
        grid_spec=pltpu.PrefetchScalarGridSpec(
            num_scalar_prefetch=1,
            grid=(2, n // size),
            in_specs=[spec(t.shape[2]) for t in terms],
            out_specs=[
                pl.BlockSpec(block, lambda i, g, _: (g * (1 - i) + last * i, 0, 0, 0)),
                pl.BlockSpec(block, lambda i, g, _: (g * i, 0, 0, 0)),
            ],
        ),
        out_shape=[jax.ShapeDtypeStruct((n, total, rows, columns), BF)] * 2,
        compiler_params=params(),
        cost_estimate=cost(SHORT),
        name="merge_halves",
    )(bit_array(step), *terms)


def whole_tiles(pieces, units):
    n_seq, _, chips, rows, half = pieces.shape
    a = pieces[:, : 1 + units].transpose(1, 0, 2, 3, 4)
    b = pieces[:, 1 + units :].transpose(0, 2, 1, 3, 4).reshape(units, -1, *a.shape[-1:])
    full = jnp.concatenate([a.reshape(1 + units, -1, half), b], axis=0)
    return full.reshape(1, 1 + 2 * units, 1, -1, half)


def body(
    tokens,
    cotangent,
    gains,
    gain_first,
    gain_second,
    mix_logits,
    logit_first,
    logit_second,
    w_value,
    value_first,
    value_second,
    w_out,
    out_first,
    out_second,
    w_up,
    up_first,
    up_second,
    w_down,
    down_first,
    down_second,
):
    head_count, length, width_pos = mix_logits.shape
    positions, seq_count, width = tokens.shape
    hidden_width = w_up.shape[1]
    token_rows = positions * seq_count
    units = hidden_width // width
    half = width // 2
    n_pos, n_seq = lax.axis_size("pos"), lax.axis_size("seq")
    pos = lax.axis_index("pos")
    pos_array = pos.astype(jnp.int32).reshape(1)
    place = jnp.stack([pos, bit_value("seq", 0)]).astype(jnp.int32)
    core = pos & 1
    core_array = core.astype(jnp.int32).reshape(1)
    chip = pos >> 1
    chips = n_pos // 2
    seq_low, pos_low = ("seq", 0), ("pos", 0)
    far = chip_bits("seq")
    across = chip_bits("pos")


    def own_piece(weight):
        rows, columns = weight.shape
        part = lax.dynamic_slice_in_dim(weight, chip * (rows // chips), rows // chips, 0)
        part = part.reshape(rows // chips, columns // width, 2, half)
        return lax.dynamic_index_in_dim(part, core, 2, keepdims=False).astype(BF)

    def both_halves(own, other):
        return jnp.where(
            core == 1,
            jnp.concatenate([other, own], axis=-1),
            jnp.concatenate([own, other], axis=-1),
        )

    away = far + across + [seq_low]
    value = Gather(own_piece(w_value)[:, 0], away, 0)
    part_rows = w_up.shape[0] // chips

    def other_pieces(out, up, down):
        a = jnp.concatenate([own_piece(out), own_piece(up)], axis=1).transpose(1, 0, 2)
        return jnp.concatenate([a, own_piece(down).reshape(units, part_rows, half)], axis=0)

    others = Gather(behind(other_pieces(w_out, w_up, w_down), (value.out,), LONG), across, 1)
    totals = row_totals(pos_array, mix_logits, n_pos, (value.out, others.out))
    totals_got = swap(totals, "pos", 1)
    for _ in across:
        others.next()
    others = others.result()
    last = others
    others = lax.all_gather(others, "seq", axis=0, tiled=False)

    tokens_rows, cot_rows = tokens.transpose(1, 0, 2), cotangent.transpose(1, 0, 2)
    tokens_wide = tokens_rows.reshape(token_rows, width).astype(F32)
    in_scale = lax.rsqrt(jnp.mean(tokens_wide * tokens_wide, axis=-1, keepdims=True) + norm_eps)
    normed_in = (tokens_wide * in_scale * gains[0]).astype(BF)
    for _ in far[1:]:
        value.next((last, totals), 1)
    for _, bit in across:
        totals = behind(totals_got, (value.out,), 1) + totals
        totals_got = swap(totals, "pos", 1 << bit)
    value.next((totals,), 1)
    for _ in across:
        value.next((normed_in,), 1)
    scale = 1.0 / (behind(totals_got, (value.out,), 1) + totals)
    attention = attention_of(pos_array, mix_logits, scale, n_pos)
    value.next((attention,), 1)
    value_half = value.result()
    value_other = swap(value_half, "pos", 1)
    value_full = both_halves(value_half, value_other)
    values = jnp.dot(normed_in, value_full, preferred_element_type=F32).astype(BF)
    values = values.reshape(seq_count, positions, width)
    parts, sent = send_to_queries(mix_forward(pos_array, attention, values, n_pos))
    others = behind(others, (sent,), 1).reshape(n_seq, 1 + 2 * units, chips, part_rows, half)
    if part_rows % 16:
        others = whole_tiles(others, units)
    others_got = swap(others, "pos", 1)
    parts[-1] = behind(parts[-1], (others,), LONG)
    (
        output,
        mixed,
        normed_mid,
        active,
        up_grad,
        grad_hidden,
        hidden_bf,
        *payloads,
        gain_mid,
    ) = feed_forward(
        core_array,
        others,
        others_got,
        tokens_rows,
        cot_rows,
        gains[1:2],
        parts,
        GROUP_HEADS,
    )

    def placed(x):
        return x.transpose(1, 0, 2)

    def rows_of(x):
        return x.reshape(*x.shape[:-3], token_rows, width)

    near = [gather_queries(part, [0])[1] for part in payloads]
    arrived = [gather_queries(part, [b for _, b in reversed(across)]) for part in payloads]
    keep_b, send_b = weight_grads(
        core_array, "grads_down", (), (rows_of(active), rows_of(cot_rows))
    )
    last = keep_b
    chains, grad_values = [], []
    keep_a = send_a = got_a = got_b = keep_w = got_w = value_terms = None
    chain = chain_a = chain_b = merged = owned = gain_total = input_grad = logits_out = None
    gain_steps = [pos_low] + across + far + [seq_low]

    def mixing_step():
        nonlocal last
        k = len(chains)
        for r in arrived[k]:
            if r:
                arrived[k][r] = behind(arrived[k][r], (last,), SHORT)
        blocks = gather_queries(None, [0], {**arrived[k], 1: near[k]})
        send, keep, grad_values_k = mix_backward(
            place,
            attention,
            values,
            [blocks[r] for r in range(n_pos)],
            sum(GROUP_HEADS[:k]),
            True,
        )
        grad_values.append(grad_values_k)
        chains.append(HalvesOut(send, keep, [seq_low] + far))
        last = send

    def grads_step():
        nonlocal keep_a, send_a, last
        keep_a, send_a = weight_grads(
            core_array,
            "grads_others",
            (rows_of(mixed), rows_of(hidden_bf)),
            (rows_of(normed_mid), behind(rows_of(up_grad), (last,), SHORT)),
        )
        last = keep_a

    def core_step():
        nonlocal got_a, got_b, last
        last = behind(send_a, (last,), SHORT)
        got_a, got_b = swap(last, "pos", 1), swap(send_b, "pos", 1)

    def input_step():
        nonlocal input_grad, gain_total, value_terms, last
        input_grad, gain_in, keep, send = input_backward(
            core_array,
            [behind(grad_values[0], (last,), SHORT), *grad_values[1:]],
            normed_in.reshape(tokens_rows.shape),
            tokens_rows,
            value_full,
            grad_hidden,
            gains[0:1],
        )
        gain_total = jnp.concatenate([gain_in, gain_mid], axis=0)
        value_terms = [keep, swap(send, "pos", 1)]
        last = keep

    def value_step():
        nonlocal value_terms, last
        value_terms[1] = behind(value_terms[1], (last,))
        for step in across:
            views = [t.reshape(-1, 2, part_rows, half) for t in value_terms]
            last, keep = halves_sum(views, step)
            value_terms = [keep, swap(last, "pos", 1 << step[1])]

    def bundle_step():
        nonlocal chain_a, chain_b, last
        dims = list(reversed(far)) + [seq_low] + list(reversed(across))
        chain_a = RowSum(keep_a, got_a, 1 + units, across + [seq_low], dims)
        chain_b = RowSum(keep_b.reshape(-1, half), got_b.reshape(-1, half), 1, across, dims)
        for _ in across:
            last = chain_a.next((last,))
        for _ in across:
            last = chain_b.next((last,))

    def projections_step():
        nonlocal chain, merged, owned, last
        owners = n_seq // 2
        if chain_a.steps:
            last = chain_a.next((last,))
        elif merged is None:
            shape = (owners, 2, -1, part_rows, half)
            terms = [
                x.reshape(shape)
                for x in (chain_b.keep, behind(chain_b.got, (last,)), *value_terms)
            ]
            last, keep = merge_halves(terms, seq_low)
            merged = [keep, swap(last, "seq", 1)]
        elif chain is None:
            a = [t.reshape(1 + units, owners, part_rows, half) for t in (chain_a.keep, chain_a.got)]
            b = [t.reshape(owners, 1 + units, part_rows, half) for t in merged]
            b[1] = behind(b[1], (last,))
            total = bundle(*a, *b)
            steps = list(far)
            step = steps.pop(0)
            left = [d for d in reversed(far)]
            view = total.reshape(1 << left.index(step), 2, -1, half)
            last, keep = halves_sum([view], step)
            left.remove(step)
            chain = RowSum(keep.reshape(-1, half), None, 1, steps, left)
            chain.got = swap(last, "seq", 1 << step[1]).reshape(-1, half)
        elif chain.steps:
            last = chain.next((last, placed(output), placed(input_grad)))
        elif owned is None:
            keep, got = (t.reshape(-1, half) for t in (chain.keep, chain.got))
            last = sum_of(keep, behind(got, (last,)))
            owned = Gather(last.reshape(2 + 2 * units, part_rows, half), list(reversed(across)), 1)
        elif owned.steps:
            owned.next((last,))
            last = owned.out

    def gain_step():
        nonlocal gain_total, last
        if gain_steps:
            axis, bit = gain_steps.pop(0)
            last = gain_total = behind(gain_total, (last,))
            gain_total = gain_total + swap(gain_total, axis, 1 << bit)

    def sum_step(k):
        nonlocal last
        if chains[k].steps:
            chains[k].next((last,))
            last = chains[k].send

    def gather_step(groups):
        nonlocal last
        for k in groups:
            while chains[k].steps:
                sum_step(k)
        pairs = [(chains[k].keep, chains[k].got) for k in groups]
        pairs[0] = (pairs[0][0], behind(pairs[0][1], (last,)))
        last = pieces_of(pairs)
        gathered[groups[0]] = lax.all_gather(last, "seq", axis=0, tiled=False)

    def update(k):
        nonlocal logits_out, last
        groups = next(g for g in parts_of if k in g)
        if groups[0] not in gathered:
            gather_step(groups)
        if k == groups[0]:
            gathered[groups[0]] = behind(gathered[groups[0]], (last,))
        logits_out = logits_adam(
            place,
            mix_logits,
            logit_first,
            logit_second,
            gathered[groups[0]],
            k - groups[0],
            sum(GROUP_HEADS[:k]),
            logits_out,
        )
        last = logits_out[0]

    steps = {
        "m": mixing_step,
        "u": grads_step,
        "c": core_step,
        "b": bundle_step,
        "w": projections_step,
        "i": input_step,
        "v": value_step,
        "g": gain_step,
    }
    for k in range(len(GROUP_HEADS)):
        steps[str(k)] = functools.partial(sum_step, k)
    gathered = {}
    parts_of = [0], list(range(1, len(GROUP_HEADS)))
    for name, k in zip("pq", parts_of):
        steps[name] = functools.partial(gather_step, k)
    for k in range(len(GROUP_HEADS)):
        steps[str(k + 3)] = functools.partial(update, k)
    for name in PLAN:
        steps[name]()
    while gain_steps:
        gain_step()
    while owned is None or owned.steps:
        projections_step()
    logits_new, logit_first_new, logit_second_new = logits_out
    owned = owned.result()
    owned = both_halves(owned, swap(owned, "pos", 1)).astype(F32)
    grad_out, grad_value = owned[0], owned[1 + 2 * units]
    grad_up = jnp.concatenate([owned[1 + j] for j in range(units)], axis=1)
    grad_down = owned[1 + units : 1 + 2 * units].reshape(units, chips, part_rows, width)
    grad_down = grad_down.transpose(1, 0, 2, 3).reshape(-1, width)
    gains_new, gain_first_new, gain_second_new = adam_update(
        gains, gain_first, gain_second, gain_total, 0.8, 0.0
    )
    value_new, value_first_new, value_second_new = adam_update(
        w_value, value_first, value_second, grad_value, 1.0 / math.sqrt(width), weight_decay
    )
    out_new, out_first_new, out_second_new = adam_update(
        w_out,
        out_first,
        out_second,
        grad_out,
        1.0 / math.sqrt(width * 16 // length),
        weight_decay,
    )
    up_new, up_first_new, up_second_new = adam_update(
        w_up, up_first, up_second, grad_up, 1.0 / math.sqrt(width), weight_decay
    )
    down_new, down_first_new, down_second_new = adam_update(
        w_down, down_first, down_second, grad_down, 1.0 / math.sqrt(hidden_width), weight_decay
    )
    return (
        placed(output),
        placed(input_grad),
        gains_new,
        gain_first_new,
        gain_second_new,
        logits_new,
        logit_first_new,
        logit_second_new,
        value_new,
        value_first_new,
        value_second_new,
        out_new,
        out_first_new,
        out_second_new,
        up_new,
        up_first_new,
        up_second_new,
        down_new,
        down_first_new,
        down_second_new,
    )


def solution(mesh):
    activations = P("pos", "seq", None)
    logits = P(None, None, "pos")
    rows = P("seq", None)
    placed = (activations,) * 2 + (P(),) * 3 + (logits,) * 3 + (rows,) * 12
    return jax.shard_map(
        body, mesh=mesh, in_specs=placed, out_specs=placed, check_vma=False
    )
```

time: 1520 us -> 517 us (0.34)
  waiting for transfers between devices: 1050 us -> 161 us
  Pallas kernels: 0 us -> 208 us
  matrix products: 140 us -> 2.54 us
  local copies, waits for them, and re-layouts: 135 us -> 37.5 us
  blocking collectives: 79.5 us -> 0 us
  other arithmetic: 86 us -> 29.2 us
  starting transfers between devices: 0.67 us -> 55.3 us
    reduce_scatter x5 -> x0, waiting for transfers between devices: 485 us -> none  [the longest x1 166 us: body(): lax.psum_scatter(grad_up, 'seq', scatter_dimension=0, tiled=True)]
    psum x2 -> x0, waiting for transfers between devices: 350 us -> none  [the longest x1 350 us: body(): logit_total = lax.psum(grad_logits, 'seq')]
    all_gather x5 -> x3, waiting for transfers between devices: 218 us -> 7.5 us  [the longest x1 7.48 us: body(): others = lax.all_gather(others, 'seq', axis=0, tiled=False)]
    pallas_call x0 -> x69, Pallas kernels: none -> 208 us  [the longest x12 39 us: halves_sum(): pl.pallas_call(halves_kernel, grid_spec=pltpu.PrefetchScalarGridSpec(num_...]
    ppermute x0 -> x47, waiting for transfers between devices: none -> 153 us  [the longest x35 122 us: swap(): return lax.ppermute(x, axis, [(i, i ^ mask) for i in range(size)])]
    dot_general x15 -> x1, matrix products: 140 us -> 2.54 us  [body(): jnp.dot(normed_in, value_full, preferred_element_type=F32).astype(BF)]
    psum x3 -> x0, blocking collectives: 65.7 us -> none  [the longest x1 43.5 us: body(): gain_total = lax.psum(jnp.stack([gain_in, gain_mid]), ('pos', 'seq'))]
    unnamed x74 -> x139, local copies, waits for them, and re-layouts: 81.5 us -> 24.8 us
  transfers between devices with their start and end apart: 12 -> 50, of which waited for: 9 -> 17; matrix products, arithmetic and copies ran while one was open for 14% -> 6% of each run, Pallas kernels for 0% -> 34%
where the time goes in v1:
time: 517 us; the launch traced here: 508 us
  Pallas kernels  208 us (40%)
  waiting for transfers between devices  161 us (31%)
  starting transfers between devices  55.3 us (11%)
  local copies, waits for them, and re-layouts  37.5 us (7%)
  other arithmetic  29.2 us (6%)
  between operations  14.8 us (3%)
    ppermute x35, waiting for transfers between devices, swap(): return lax.ppermute(x, axis, [(i, i ^ mask) for i in range(size)])  122 us
    pallas_call x12, Pallas kernels, halves_sum(): pl.pallas_call(halves_kernel, grid_spec=pltpu.PrefetchScalarGridSpec(num_...  39 us
    pallas_call x1, Pallas kernels, feed_forward(): pl.pallas_call(functools.partial(ffn_kernel, len(parts)), grid_spec=pltpu...  37 us
    pallas_call x3, Pallas kernels, logits_adam(): pl.pallas_call(logits_adam_kernel, grid_spec=pltpu.PrefetchScalarGridSpec...  33.1 us
    ppermute x35, starting transfers between devices, swap(): return lax.ppermute(x, axis, [(i, i ^ mask) for i in range(size)])  32 us
    unnamed x139, local copies, waits for them, and re-layouts  24.8 us
    pallas_call x3, Pallas kernels, mix_backward(): pl.pallas_call(functools.partial(backward_kernel, blocks, split), grid_sp...  23.8 us
    ppermute x3, waiting for transfers between devices, send_to_queries(): got = lax.ppermute(sent, 'pos', pairs)  22.9 us
  transfers between devices with their start and end apart: 50, of which 17 were waited for; matrix products, arithmetic and copies ran while one was open for 6% of the time, Pallas kernels for 34%

profile of v1, /device:TPU:0, one launch (start us, length us, event | category | flops | bytes accessed | tf_op | source)
XLA Modules:
  0.0 507.9 jit_solution(10542584043465581595)
XLA Ops:
  16.9 8.0 %collective-permute-done = bf16[9,48,384]{2,1,0:T(8,128)(2,1)S(1)} collective-permute-done((bf16[9,48,384]{2,1,0:T(8,128)(2,1)}, bf16[9,48,384]{2,1,0:T(8,128)(2,1)S(1)}, u32[]{:S(2)}, u32[]{:S(2)}) %collective-permute-start) | collective-permute-done | bytes 331808 | tf_op jit(solution)/shard_map/ppermute | solution.py:45
  29.0 8.7 %row_totals.1.refs_2_ = f32[16,1024]{1,0:T(8,128)} custom-call(s32[1]{0:T(128)} %bitcast.8.pos_ref, f32[12,1024,256]{2,1,0:T(8,128)} %weight_ref.5, bf16[48,384]{1,0:T(8,128)(2,1)} %bitcast.198, bf16[9,48,384]{2,1,0:T(8,128)(2,1)} %behind.39.refs_1_), custom_call_target="tpu_custom_call" | custom-call | flops 500000000 | tf_op jit(solution)/shard_map/row_totals/pallas_call | solution.py:324
  47.9 7.6 %collective-permute-done.4.refs_0_ = bf16[2,48,384]{2,1,0:T(8,128)(2,1)S(1)} collective-permute-done((bf16[2,48,384]{2,1,0:T(8,128)(2,1)S(1)}, bf16[2,48,384]{2,1,0:T(8,128)(2,1)S(1)}, u32[]{:S(2)}, u32[]{:S(2)}) %collective-permute-start.4) | collective-permute-done | bytes 73760 | tf_op jit(solution)/shard_map/ppermute | solution.py:45
  59.1 3.8 collective-permute-done.5.refs_0_
  68.4 10.8 %attention.1.refs_1_.attention_ref = bf16[12,1024,256]{2,1,0:T(8,128)(2,1)} custom-call(s32[1]{0:T(128)} %bitcast.8.pos_ref, f32[12,1024,256]{2,1,0:T(8,128)} %weight_ref.5, f32[16,1024]{1,0:T(8,128)} %add_divide_fusion.scale_ref), custom_call_target="tpu_custom_call" | custom-call | flops 500000000 | tf_op jit(solution)/shard_map/attention/pallas_call | solution.py:365
  86.0 9.1 %mix_forward.1 = (bf16[4,256,768]{2,1,0:T(8,128)(2,1)}, bf16[4,256,768]{2,1,0:T(8,128)(2,1)}, bf16[4,256,768]{2,1,0:T(8,128)(2,1)}, bf16[4,256,768]{2,1,0:T(8,128)(2,1)}) custom-call(s32[1]{0:T(128)} %bitcast.8.pos_ref, bf16[12,1024,256]{2,1,0:T(8,128)(2,1)} %attention.1.refs_1_.attention_ref, bf16[4,256,768]{2,1,0:T(8,128)(2,1)} %bitcast.192), custom_call_target="tpu_custom_call" | custom-call | flops 500000000 | tf_op jit(solution)/shard_map/mix_forward/pallas_call | solution.py:409
  97.1 3.5 collective-permute-done.8
  108.0 3.3 collective-permute-start.10
  111.3 7.5 %all-gather.6.cloned.1.call-done.refs_0_ = bf16[8,9,96,384]{3,2,1,0:T(8,128)(2,1)} async-done(((bf16[1,9,96,384]{3,2,1,0:T(8,128)(2,1)}), bf16[8,9,96,384]{3,2,1,0:T(8,128)(2,1)}) %all-gather.6.cloned.1.call-update) | async-done | bytes 5308432 | tf_op jit(solution)/shard_map/all_gather | solution.py:1027
  118.8 19.4 %collective-permute-done.11.refs_0_ = bf16[4,256,768]{2,1,0:T(8,128)(2,1)} collective-permute-done((bf16[4,256,768]{2,1,0:T(8,128)(2,1)S(1)}, bf16[4,256,768]{2,1,0:T(8,128)(2,1)}, u32[]{:S(2)}, u32[]{:S(2)}) %collective-permute-start.11) | collective-permute-done | bytes 1572896 | tf_op jit(solution)/shard_map/ppermute | solution.py:248
  138.3 37.0 %feed_forward.1 = (bf16[4,256,768]{2,1,0:T(8,128)(2,1)}, bf16[4,256,768]{2,1,0:T(8,128)(2,1)}, bf16[4,256,768]{2,1,0:T(8,128)(2,1)}, bf16[4,4,256,768]{3,2,1,0:T...) custom-call(s32[1]{0:T(128)} %bitcast.core_ref, ...), custom_call_target="tpu_custom_call" | custom-call | flops 8000000000 | tf_op jit(solution)/shard_map/feed_forward/pallas_call | solution.py:560
  177.8 9.6 %grads_down.1 = (bf16[4,768,384]{2,1,0:T(8,128)(2,1)}, bf16[4,768,384]{2,1,0:T(8,128)(2,1)}) custom-call(s32[1]{0:T(128)} %bitcast.core_ref, bf16[4,1024,768]{2,1,0:T(8,128)(2,1)} %bitcast.244, bf16[1024,768]{1,0:T(8,128)(2,1)} %bitcast.191), custom_call_target="tpu_custom_call" | custom-call | flops 8000000000 | tf_op jit(solution)/shard_map/grads_down/pallas_call | solution.py:627
  187.4 3.8 collective-permute-done.13.refs_0_
  198.8 7.9 %mix_backward.3 = (bf16[2,4,256,256]{3,2,1,0:T(8,128)(2,1)}, bf16[2,4,256,256]{3,2,1,0:T(8,128)(2,1)}, bf16[4,256,256]{2,1,0:T(8,128)(2,1)}) custom-call(s32[2]{0:T(128)} %pad_add_fusion.place_ref, bf16[12,1024,256]{2,1,0:T(8,128)(2,1)} %attention.1.refs_1_.attention_ref, bf16[4,256,768]{2,1,0:T(8,128)(2,1)} %bitcast.193, ...), custom_call_target="tpu_custom_call" | custom-call | flops 199999995904 | tf_op jit(solution)/shard_map/mix_backward/pallas_call | solution.py:722
  206.7 4.6 collective-permute-done.17.refs_0_
  217.8 7.9 %mix_backward.4 = (bf16[2,4,256,256]{3,2,1,0:T(8,128)(2,1)}, bf16[2,4,256,256]{3,2,1,0:T(8,128)(2,1)}, bf16[4,256,256]{2,1,0:T(8,128)(2,1)}) custom-call(s32[2]{0:T(128)} %pad_add_fusion.place_ref, bf16[12,1024,256]{2,1,0:T(8,128)(2,1)} %attention.1.refs_1_.attention_ref, bf16[4,256,768]{2,1,0:T(8,128)(2,1)} %bitcast.194, ...), custom_call_target="tpu_custom_call" | custom-call | flops 199999995904 | tf_op jit(solution)/shard_map/mix_backward/pallas_call | solution.py:722
  225.7 12.3 %grads_others.1 = (bf16[5,768,384]{2,1,0:T(8,128)(2,1)}, bf16[5,768,384]{2,1,0:T(8,128)(2,1)}) custom-call(s32[1]{0:T(128)} %bitcast.core_ref, bf16[1024,768]{1,0:T(8,128)(2,1)} %bitcast.247, bf16[1024,768]{1,0:T(8,128)(2,1)} %bitcast.249, bf16[1024,768]{1,0:T(8,128)(2,1)} %bitcast.248, bf16[4,1024,768]{2,1,0:T(8,128)(2,1)} %behind.50.refs_3_), custom_call_target="tpu_custom_call" | custom-call | flops 8000000000 | tf_op jit(solution)/shard_map/grads_others/pallas_call | solution.py:627
  238.0 3.4 collective-permute-done.15.refs_0_
  250.9 8.0 %mix_backward.5 = (bf16[2,4,256,256]{3,2,1,0:T(8,128)(2,1)}, bf16[2,4,256,256]{3,2,1,0:T(8,128)(2,1)}, bf16[4,256,256]{2,1,0:T(8,128)(2,1)}) custom-call(s32[2]{0:T(128)} %pad_add_fusion.place_ref, bf16[12,1024,256]{2,1,0:T(8,128)(2,1)} %attention.1.refs_1_.attention_ref, bf16[4,256,768]{2,1,0:T(8,128)(2,1)} %bitcast.195, ...), custom_call_target="tpu_custom_call" | custom-call | flops 199999995904 | tf_op jit(solution)/shard_map/mix_backward/pallas_call | solution.py:722
  260.0 7.2 %halves_sum.13 = (bf16[40,48,384]{2,1,0:T(8,128)(2,1)}, bf16[40,48,384]{2,1,0:T(8,128)(2,1)}) custom-call(s32[1]{0:T(128)} %bitcast.42.bit_ref, bf16[40,2,48,384]{3,2,1,0:T(8,128)(2,1)} %bitcast.245, bf16[40,2,48,384]{3,2,1,0:T(8,128)(2,1)} %bitcast.46.refs_1_), custom_call_target="tpu_custom_call" | custom-call | flops 8000000000 | tf_op jit(solution)/shard_map/halves_sum/pallas_call | solution.py:142
  267.6 6.7 %halves_sum.14 = (bf16[8,192,384]{2,1,0:T(8,128)(2,1)}, bf16[8,192,384]{2,1,0:T(8,128)(2,1)}) custom-call(s32[1]{0:T(128)} %bitcast.42.bit_ref, bf16[8,2,192,384]{3,2,1,0:T(8,128)(2,1)} %bitcast.246, bf16[8,2,192,384]{3,2,1,0:T(8,128)(2,1)} %bitcast.47.refs_1_), custom_call_target="tpu_custom_call" | custom-call | flops 8000000000 | tf_op jit(solution)/shard_map/halves_sum/pallas_call | solution.py:142
  281.3 8.7 %input_backward.1 = (bf16[4,256,768]{2,1,0:T(8,128)(2,1)}, f32[1,768]{1,0:T(1,128)}, bf16[1,768,384]{2,1,0:T(8,128)(2,1)}, bf16[1,768,384]{2,1,0:T(8,128)(2,1)}) custom-call(s32[1]{0:T(128)} %bitcast.core_ref, bf16[4,256,256]{2,1,0:T(8,128)(2,1)} %behind.57.refs_0_, bf16[4,256,256]{2,1,0:T(8,128)(2,1)} %get-tuple-element.114.refs_1_, ...), custom_call_target="tpu_custom_call" | custom-call | flops 8000000000 | tf_op jit(solution)/shard_map/input_backward/pallas_call | solution.py:860
  296.5 7.9 %collective-permute-done.27.refs_0_ = bf16[1024,256]{1,0:T(8,128)(2,1)} collective-permute-done((bf16[1024,256]{1,0:T(8,128)(2,1)}, bf16[1024,256]{1,0:T(8,128)(2,1)}, u32[]{:S(2)}, u32[]{:S(2)}) %collective-permute-start.27) | collective-permute-done | bytes 524320 | tf_op jit(solution)/shard_map/ppermute | solution.py:45
  321.3 22.2 %collective-permute-done.32.refs_0_ = bf16[1024,256]{1,0:T(8,128)(2,1)S(1)} collective-permute-done((bf16[1024,256]{1,0:T(8,128)(2,1)}, bf16[1024,256]{1,0:T(8,128)(2,1)S(1)}, u32[]{:S(2)}, u32[]{:S(2)}) %collective-permute-start.32) | collective-permute-done | bytes 524320 | tf_op jit(solution)/shard_map/ppermute | solution.py:45
  347.4 6.0 %merge_halves.1 = (bf16[4,5,48,384]{3,2,1,0:T(8,128)(2,1)}, bf16[4,5,48,384]{3,2,1,0:T(8,128)(2,1)}) custom-call(s32[1]{0:T(128)} %bitcast.28.bit_ref, bf16[4,2,4,48,384]{4,3,2,1,0:T(8,128)(2,1)} %bitcast.252, bf16[4,2,4,48,384]{4,3,2,1,0:T(8,128)(2,1)} %bitcast.71.got, bf16[4,2,1,48,384]{4,3,2,1,0:T(8,128)(2,1)} %bitcast.263, ...), custom_call_target="tpu_custom_call" | custom-call | flops 8000000000 | tf_op jit(solution)/shard_map/merge_halves/pallas_call | solution.py:932
  359.2 6.7 %collective-permute-done.39.refs_3_ = bf16[512,256]{1,0:T(8,128)(2,1)S(1)} collective-permute-done((bf16[512,256]{1,0:T(8,128)(2,1)}, bf16[512,256]{1,0:T(8,128)(2,1)S(1)}, u32[]{:S(2)}, u32[]{:S(2)}) %collective-permute-start.39) | collective-permute-done | bytes 262176 | tf_op jit(solution)/shard_map/ppermute | solution.py:45
  368.7 11.2 %logits_adam.3 = (f32[12,1024,256]{2,1,0:T(8,128)}, f32[12,1024,256]{2,1,0:T(8,128)}, f32[12,1024,256]{2,1,0:T(8,128)}) custom-call(s32[2]{0:T(128)} %pad_add_fusion.place_ref, f32[12,1024,256]{2,1,0:T(8,128)} %weight_ref.5, f32[12,1024,256]{2,1,0:T(8,128)} %first_ref.5, f32[12,1024,256]{2,1,0:T(8,128)} %second_ref.5, ...), custom_call_target="tpu_custom_call" | custom-call | flops 20000000000 | tf_op jit(solution)/shard_map/logits_adam/pallas_call | solution.py:807
  381.7 4.0 bundle.1
  395.0 17.5 %collective-permute-done.40 = f32[2,768]{1,0:T(2,128)S(1)} collective-permute-done((f32[2,768]{1,0:T(2,128)}, f32[2,768]{1,0:T(2,128)S(1)}, u32[]{:S(2)}, u32[]{:S(2)}) %collective-permute-start.40) | collective-permute-done | bytes 6176 | tf_op jit(solution)/shard_map/ppermute | solution.py:45
  419.2 38.7 %collective-permute-done.42 = f32[2,768]{1,0:T(2,128)S(1)} collective-permute-done((f32[2,768]{1,0:T(2,128)}, f32[2,768]{1,0:T(2,128)S(1)}, u32[]{:S(2)}, u32[]{:S(2)}) %collective-permute-start.42) | collective-permute-done | bytes 6176 | tf_op jit(solution)/shard_map/ppermute | solution.py:45
  467.2 10.9 %logits_adam.4 = (f32[12,1024,256]{2,1,0:T(8,128)}, f32[12,1024,256]{2,1,0:T(8,128)}, f32[12,1024,256]{2,1,0:T(8,128)}) custom-call(s32[2]{0:T(128)} %pad_add_fusion.place_ref, f32[12,1024,256]{2,1,0:T(8,128)} %weight_ref.5, f32[12,1024,256]{2,1,0:T(8,128)} %first_ref.5, ...), custom_call_target="tpu_custom_call", output_to_operand_aliasing={{0}: (8, {}), {1}: (9, {}), {2}: (10, {})} | custom-call | flops 20000000000 | tf_op jit(solution)/shard_map/logits_adam/pallas_call | solution.py:807
  480.3 11.0 %logits_adam.5 = (f32[12,1024,256]{2,1,0:T(8,128)}, f32[12,1024,256]{2,1,0:T(8,128)}, f32[12,1024,256]{2,1,0:T(8,128)}) custom-call(s32[2]{0:T(128)} %pad_add_fusion.place_ref, f32[12,1024,256]{2,1,0:T(8,128)} %weight_ref.5, f32[12,1024,256]{2,1,0:T(8,128)} %first_ref.5, ...), custom_call_target="tpu_custom_call", output_to_operand_aliasing={{0}: (8, {}), {1}: (9, {}), {2}: (10, {})} | custom-call | flops 20000000000 | tf_op jit(solution)/shard_map/logits_adam/pallas_call | solution.py:807
  (333 shorter events, 158.1 us)
Async XLA Ops:
  7.2 111.6 %all-gather.6.cloned.1.call-start = ((), (), s32[]{:S(2)}) async-start(), calls=%async_computation | async-start | bytes 5971968 | tf_op jit(solution)/shard_map/all_gather | solution.py:1027
  27.1 341.6 %all-gather.8.cloned.1.call-start = ((), (), s32[]{:S(2)}) async-start(), calls=%async_computation.1 | async-start | bytes 2359296 | tf_op jit(solution)/shard_map/all_gather | solution.py:1217
  47.3 19.0 %collective-permute-start.3 = (f32[16,1024]{1,0:T(8,128)S(1)}, f32[16,1024]{1,0:T(8,128)S(1)}, u32[]{:S(2)}, u32[]{:S(2)}) collective-permute-start(f32[16,1024]{1,0:T(8,128)S(1)} %add.126.refs_1_), channel_id=1, source_target_pairs={{0,16},{8,24},{16,0},{24,8},{1,17},{9,25},{17,1},{25,9},{2,18},{10... | collective-permute-start | bytes 196616 | tf_op jit(solution)/shard_map/ppermute | solution.py:45
  64.7 14.5 %collective-permute-start.6 = (bf16[2,2,2,48,384]{4,3,2,1,0:T(8,128)(2,1)S(1)}, bf16[2,2,2,48,384]{4,3,2,1,0:T(8,128)(2,1)S(1)}, u32[]{:S(2)}, u32[]{:S(2)}) collective-permute-start(bf16[2,2,2,48,384]{4,3,2,1,0:T(8,128)(2,1)S(1)} %maximum_select_fusion.5.refs_1_), channel_id=1, source_target_pairs={{0,1},{1,0},{2,3},{3,2},{4,5},{5,4},{6,7},{7,6},{8,9},{9,8},{10,11... | collective-permute-start | bytes 884744 | tf_op jit(solution)/shard_map/ppermute | solution.py:45
  102.5 35.8 %collective-permute-start.11 = (bf16[4,256,768]{2,1,0:T(8,128)(2,1)S(1)}, bf16[4,256,768]{2,1,0:T(8,128)(2,1)}, u32[]{:S(2)}, u32[]{:S(2)}) collective-permute-start(bf16[4,256,768]{2,1,0:T(8,128)(2,1)S(1)} %add_convert_fusion.refs_1_), channel_id=1, source_target_pairs={{0,16},{8,24},{1,17},{9,25},{2,18},{10,26},{3,19},{11,27},{4,20},{... | collective-permute-start | bytes 4718600 | tf_op jit(solution)/shard_map/ppermute | solution.py:248
  108.0 30.3 %collective-permute-start.10 = (bf16[4,256,768]{2,1,0:T(8,128)(2,1)}, bf16[4,256,768]{2,1,0:T(8,128)(2,1)}, u32[]{:S(2)}, u32[]{:S(2)}) collective-permute-start(bf16[4,256,768]{2,1,0:T(8,128)(2,1)} %get-tuple-element.90), channel_id=1, source_target_pairs={{0,8},{16,24},{1,9},{17,25},{2,10},{18,26},{3,11},{19,27},{4,12},{... | collective-permute-start | bytes 4718600 | tf_op jit(solution)/shard_map/ppermute | solution.py:248
  118.8 19.5 %collective-permute-start.9 = (bf16[8,9,2,48,384]{4,3,2,1,0:T(8,128)(2,1)}, bf16[8,9,2,48,384]{4,3,2,1,0:T(8,128)(2,1)}, u32[]{:S(2)}, u32[]{:S(2)}) collective-permute-start(bf16[8,9,2,48,384]{4,3,2,1,0:T(8,128)(2,1)} %bitcast.173), channel_id=1, source_target_pairs={{0,8},{8,0},{16,24},{24,16},{1,9},{9,1},{17,25},{25,17},{2,10},{10... | collective-permute-start | bytes 15925256 | tf_op jit(solution)/shard_map/ppermute | solution.py:45
  175.2 16.0 %collective-permute-start.13 = (bf16[1,1040,256]{2,1,0:T(8,128)(2,1)}, bf16[1,1040,256]{2,1,0:T(8,128)(2,1)S(1)}, u32[]{:S(2)}, u32[]{:S(2)}) collective-permute-start(bf16[1,1040,256]{2,1,0:T(8,128)(2,1)} %get-tuple-element.92.refs_0_.refs_4_), channel_id=1, source_target_pairs={{16,0},{24,8},{17,1},{25,9},{18,2},{26,10},{19,3},{27,11},{20,4},{... | collective-permute-start | bytes 1597448 | tf_op jit(solution)/shard_map/ppermute | solution.py:267
  176.5 20.6 %collective-permute-start.12 = (bf16[1,1040,256]{2,1,0:T(8,128)(2,1)}, bf16[1,1040,256]{2,1,0:T(8,128)(2,1)S(1)}, u32[]{:S(2)}, u32[]{:S(2)}) collective-permute-start(bf16[1,1040,256]{2,1,0:T(8,128)(2,1)} %get-tuple-element.92.refs_0_.refs_4_), channel_id=1, source_target_pairs={{8,0},{24,16},{9,1},{25,17},{10,2},{26,18},{11,3},{27,19},{12,4},{... | collective-permute-start | bytes 1597448 | tf_op jit(solution)/shard_map/ppermute | solution.py:267
  194.6 16.7 %collective-permute-start.17 = (bf16[1,1040,256]{2,1,0:T(8,128)(2,1)}, bf16[1,1040,256]{2,1,0:T(8,128)(2,1)}, u32[]{:S(2)}, u32[]{:S(2)}) collective-permute-start(bf16[1,1040,256]{2,1,0:T(8,128)(2,1)} %get-tuple-element.102.refs_0_.refs_4_), channel_id=1, source_target_pairs={{16,0},{24,8},{17,1},{25,9},{18,2},{26,10},{19,3},{27,11},{20,4},{... | collective-permute-start | bytes 1597448 | tf_op jit(solution)/shard_map/ppermute | solution.py:267
  195.9 21.1 %collective-permute-start.16 = (bf16[1,1040,256]{2,1,0:T(8,128)(2,1)}, bf16[1,1040,256]{2,1,0:T(8,128)(2,1)}, u32[]{:S(2)}, u32[]{:S(2)}) collective-permute-start(bf16[1,1040,256]{2,1,0:T(8,128)(2,1)} %get-tuple-element.102.refs_0_.refs_4_), channel_id=1, source_target_pairs={{8,0},{24,16},{9,1},{25,17},{10,2},{26,18},{11,3},{27,19},{12,4},{... | collective-permute-start | bytes 1597448 | tf_op jit(solution)/shard_map/ppermute | solution.py:267
  213.2 31.0 %collective-permute-start.23 = (bf16[1,1040,256]{2,1,0:T(8,128)(2,1)}, bf16[1,1040,256]{2,1,0:T(8,128)(2,1)}, u32[]{:S(2)}, u32[]{:S(2)}) collective-permute-start(bf16[1,1040,256]{2,1,0:T(8,128)(2,1)} %get-tuple-element.109.refs_0_.refs_4_), channel_id=1, source_target_pairs={{16,0},{24,8},{17,1},{25,9},{18,2},{26,10},{19,3},{27,11},{20,4},{... | collective-permute-start | bytes 1597448 | tf_op jit(solution)/shard_map/ppermute | solution.py:267
  214.5 35.6 %collective-permute-start.22 = (bf16[1,1040,256]{2,1,0:T(8,128)(2,1)}, bf16[1,1040,256]{2,1,0:T(8,128)(2,1)}, u32[]{:S(2)}, u32[]{:S(2)}) collective-permute-start(bf16[1,1040,256]{2,1,0:T(8,128)(2,1)} %get-tuple-element.109.refs_0_.refs_4_), channel_id=1, source_target_pairs={{8,0},{24,16},{9,1},{25,17},{10,2},{26,18},{11,3},{27,19},{12,4},{... | collective-permute-start | bytes 1597448 | tf_op jit(solution)/shard_map/ppermute | solution.py:267
  216.0 25.4 %collective-permute-start.15 = (bf16[2048,256]{1,0:T(8,128)(2,1)}, bf16[2048,256]{1,0:T(8,128)(2,1)}, u32[]{:S(2)}, u32[]{:S(2)}) collective-permute-start(bf16[2048,256]{1,0:T(8,128)(2,1)} %bitcast.34), channel_id=1, source_target_pairs={{0,1},{1,0},{2,3},{3,2},{4,5},{5,4},{6,7},{7,6},{8,9},{9,8},{10,11... | collective-permute-start | bytes 3145736 | tf_op jit(solution)/shard_map/ppermute | solution.py:45
  248.7 18.9 %collective-permute-start.20 = (bf16[4,768,384]{2,1,0:T(8,128)(2,1)}, bf16[4,768,384]{2,1,0:T(8,128)(2,1)}, u32[]{:S(2)}, u32[]{:S(2)}) collective-permute-start(bf16[4,768,384]{2,1,0:T(8,128)(2,1)} %get-tuple-element.108), channel_id=1, source_target_pairs={{0,8},{8,0},{16,24},{24,16},{1,9},{9,1},{17,25},{25,17},{2,10},{10... | collective-permute-start | bytes 7077896 | tf_op jit(solution)/shard_map/ppermute | solution.py:45
  249.2 40.9 %collective-permute-start.26 = (bf16[2048,256]{1,0:T(8,128)(2,1)}, bf16[2048,256]{1,0:T(8,128)(2,1)}, u32[]{:S(2)}, u32[]{:S(2)}) collective-permute-start(bf16[2048,256]{1,0:T(8,128)(2,1)} %bitcast.53), channel_id=1, source_target_pairs={{0,1},{1,0},{2,3},{3,2},{4,5},{5,4},{6,7},{7,6},{8,9},{9,8},{10,11... | collective-permute-start | bytes 3145736 | tf_op jit(solution)/shard_map/ppermute | solution.py:45
  250.1 25.9 %collective-permute-start.19 = (bf16[1024,256]{1,0:T(8,128)(2,1)}, bf16[1024,256]{1,0:T(8,128)(2,1)}, u32[]{:S(2)}, u32[]{:S(2)}) collective-permute-start(bf16[1024,256]{1,0:T(8,128)(2,1)} %bitcast.41.refs_1_), channel_id=1, source_target_pairs={{0,2},{1,3},{2,0},{3,1},{4,6},{5,7},{6,4},{7,5},{8,10},{9,11},{10,... | collective-permute-start | bytes 1572872 | tf_op jit(solution)/shard_map/ppermute | solution.py:45
  258.9 51.9 %collective-permute-start.31 = (bf16[2048,256]{1,0:T(8,128)(2,1)}, bf16[2048,256]{1,0:T(8,128)(2,1)S(1)}, u32[]{:S(2)}, u32[]{:S(2)}) collective-permute-start(bf16[2048,256]{1,0:T(8,128)(2,1)} %bitcast.225), channel_id=1, source_target_pairs={{0,1},{1,0},{2,3},{3,2},{4,5},{5,4},{6,7},{7,6},{8,9},{9,8},{10,11... | collective-permute-start | bytes 3145736 | tf_op jit(solution)/shard_map/ppermute | solution.py:45
  267.2 49.0 %collective-permute-start.33 = (bf16[40,48,384]{2,1,0:T(8,128)(2,1)}, bf16[40,48,384]{2,1,0:T(8,128)(2,1)S(1)}, u32[]{:S(2)}, u32[]{:S(2)}) collective-permute-start(bf16[40,48,384]{2,1,0:T(8,128)(2,1)} %get-tuple-element.111.refs_1_), channel_id=1, source_target_pairs={{0,16},{8,24},{16,0},{24,8},{1,17},{9,25},{17,1},{25,9},{2,18},{10... | collective-permute-start | bytes 4423688 | tf_op jit(solution)/shard_map/ppermute | solution.py:45
  274.4 72.4 %collective-permute-start.30 = (bf16[8,192,384]{2,1,0:T(8,128)(2,1)}, bf16[8,192,384]{2,1,0:T(8,128)(2,1)}, u32[]{:S(2)}, u32[]{:S(2)}) collective-permute-start(bf16[8,192,384]{2,1,0:T(8,128)(2,1)} %get-tuple-element.112.refs_1_), channel_id=1, source_target_pairs={{0,16},{8,24},{16,0},{24,8},{1,17},{9,25},{17,1},{25,9},{2,18},{10... | collective-permute-start | bytes 3538952 | tf_op jit(solution)/shard_map/ppermute | solution.py:45
  278.1 15.5 %collective-permute-start.28 = (bf16[512,256]{1,0:T(8,128)(2,1)}, bf16[512,256]{1,0:T(8,128)(2,1)S(1)}, u32[]{:S(2)}, u32[]{:S(2)}) collective-permute-start(bf16[512,256]{1,0:T(8,128)(2,1)} %bitcast.241), channel_id=1, source_target_pairs={{0,4},{1,5},{2,6},{3,7},{4,0},{5,1},{6,2},{7,3},{8,12},{9,13},{10,... | collective-permute-start | bytes 786440 | tf_op jit(solution)/shard_map/ppermute | solution.py:45
  296.1 171.1 %all-gather.10.cloned.1.call-start = ((), (), s32[]{:S(2)}) async-start(), calls=%async_computation.2 | async-start | bytes 4718592 | tf_op jit(solution)/shard_map/all_gather | solution.py:1217
  306.6 48.2 %collective-permute-start.38 = (bf16[512,256]{1,0:T(8,128)(2,1)}, bf16[512,256]{1,0:T(8,128)(2,1)S(1)}, u32[]{:S(2)}, u32[]{:S(2)}) collective-permute-start(bf16[512,256]{1,0:T(8,128)(2,1)} %bitcast.237), channel_id=1, source_target_pairs={{0,4},{1,5},{2,6},{3,7},{4,0},{5,1},{6,2},{7,3},{8,12},{9,13},{10,... | collective-permute-start | bytes 786440 | tf_op jit(solution)/shard_map/ppermute | solution.py:45
  309.1 37.6 %collective-permute-start.34 = (bf16[8,48,384]{2,1,0:T(8,128)(2,1)}, bf16[8,48,384]{2,1,0:T(8,128)(2,1)S(1)}, u32[]{:S(2)}, u32[]{:S(2)}) collective-permute-start(bf16[8,48,384]{2,1,0:T(8,128)(2,1)} %get-tuple-element.127.refs_1_), channel_id=1, source_target_pairs={{0,16},{8,24},{16,0},{24,8},{1,17},{9,25},{17,1},{25,9},{2,18},{10... | collective-permute-start | bytes 884744 | tf_op jit(solution)/shard_map/ppermute | solution.py:45
  314.6 28.9 %collective-permute-start.32 = (bf16[1024,256]{1,0:T(8,128)(2,1)}, bf16[1024,256]{1,0:T(8,128)(2,1)S(1)}, u32[]{:S(2)}, u32[]{:S(2)}) collective-permute-start(bf16[1024,256]{1,0:T(8,128)(2,1)} %bitcast.232), channel_id=1, source_target_pairs={{0,2},{1,3},{2,0},{3,1},{4,6},{5,7},{6,4},{7,5},{8,10},{9,11},{10,... | collective-permute-start | bytes 1572872 | tf_op jit(solution)/shard_map/ppermute | solution.py:45
  320.6 60.2 %collective-permute-start.36 = (bf16[20,48,384]{2,1,0:T(8,128)(2,1)}, bf16[20,48,384]{2,1,0:T(8,128)(2,1)S(1)}, u32[]{:S(2)}, u32[]{:S(2)}) collective-permute-start(bf16[20,48,384]{2,1,0:T(8,128)(2,1)} %get-tuple-element.133.refs_1_), channel_id=1, source_target_pairs={{0,1},{1,0},{2,3},{3,2},{4,5},{5,4},{6,7},{7,6},{8,9},{9,8},{10,11... | collective-permute-start | bytes 2211848 | tf_op jit(solution)/shard_map/ppermute | solution.py:45
  346.3 19.6 %collective-permute-start.39 = (bf16[512,256]{1,0:T(8,128)(2,1)}, bf16[512,256]{1,0:T(8,128)(2,1)S(1)}, u32[]{:S(2)}, u32[]{:S(2)}) collective-permute-start(bf16[512,256]{1,0:T(8,128)(2,1)} %bitcast.239), channel_id=1, source_target_pairs={{0,4},{1,5},{2,6},{3,7},{4,0},{5,1},{6,2},{7,3},{8,12},{9,13},{10,... | collective-permute-start | bytes 786440 | tf_op jit(solution)/shard_map/ppermute | solution.py:45
  353.4 26.5 %collective-permute-start.37 = (bf16[4,5,48,384]{3,2,1,0:T(8,128)(2,1)}, bf16[4,5,48,384]{3,2,1,0:T(8,128)(2,1)S(1)}, u32[]{:S(2)}, u32[]{:S(2)}) collective-permute-start(bf16[4,5,48,384]{3,2,1,0:T(8,128)(2,1)} %get-tuple-element.136.refs_1_), channel_id=1, source_target_pairs={{0,1},{1,0},{2,3},{3,2},{4,5},{5,4},{6,7},{7,6},{8,9},{9,8},{10,11... | collective-permute-start | bytes 2211848 | tf_op jit(solution)/shard_map/ppermute | solution.py:45
  388.2 24.9 %collective-permute-start.41 = (bf16[2,480,384]{2,1,0:T(8,128)(2,1)}, bf16[2,480,384]{2,1,0:T(8,128)(2,1)S(1)}, u32[]{:S(2)}, u32[]{:S(2)}) collective-permute-start(bf16[2,480,384]{2,1,0:T(8,128)(2,1)} %get-tuple-element.142.refs_1_), channel_id=1, source_target_pairs={{0,2},{1,3},{2,0},{3,1},{4,6},{5,7},{6,4},{7,5},{8,10},{9,11},{10,... | collective-permute-start | bytes 2211848 | tf_op jit(solution)/shard_map/ppermute | solution.py:45
  388.9 23.6 %collective-permute-start.40 = (f32[2,768]{1,0:T(2,128)}, f32[2,768]{1,0:T(2,128)S(1)}, u32[]{:S(2)}, u32[]{:S(2)}) collective-permute-start(f32[2,768]{1,0:T(2,128)} %behind.71.refs_1_), channel_id=1, source_target_pairs={{0,2},{1,3},{2,0},{3,1},{4,6},{5,7},{6,4},{7,5},{8,10},{9,11},{10,... | collective-permute-start | bytes 18440 | tf_op jit(solution)/shard_map/ppermute | solution.py:45
  416.3 42.9 %collective-permute-start.43 = (bf16[1,480,384]{2,1,0:T(8,128)(2,1)}, bf16[1,480,384]{2,1,0:T(8,128)(2,1)S(1)}, u32[]{:S(2)}, u32[]{:S(2)}) collective-permute-start(bf16[1,480,384]{2,1,0:T(8,128)(2,1)} %get-tuple-element.144.refs_1_), channel_id=1, source_target_pairs={{0,4},{1,5},{2,6},{3,7},{4,0},{5,1},{6,2},{7,3},{8,12},{9,13},{10,... | collective-permute-start | bytes 1105928 | tf_op jit(solution)/shard_map/ppermute | solution.py:45
  418.7 39.2 %collective-permute-start.42 = (f32[2,768]{1,0:T(2,128)}, f32[2,768]{1,0:T(2,128)S(1)}, u32[]{:S(2)}, u32[]{:S(2)}) collective-permute-start(f32[2,768]{1,0:T(2,128)} %behind.73.refs_1_), channel_id=1, source_target_pairs={{0,4},{1,5},{2,6},{3,7},{4,0},{5,1},{6,2},{7,3},{8,12},{9,13},{10,... | collective-permute-start | bytes 18440 | tf_op jit(solution)/shard_map/ppermute | solution.py:45
  (84 other events, 315.7 us)
Sparse Core Ops, SparseCore 0:
  27.2 91.5 all-gather.5
  296.2 69.1 all-gather.7
  368.8 97.5 all-gather.9

commit v2 on v1

--- a/solution.py
+++ b/solution.py
@@ -1021,7 +1021,7 @@
     totals = row_totals(pos_array, mix_logits, n_pos, (value.out, others.out))
     totals_got = swap(totals, "pos", 1)
     for _ in across:
-        others.next()
+        others.next((totals,), FRONT)
     others = others.result()
     last = others
     others = lax.all_gather(others, "seq", axis=0, tiled=False)

time: 517 us -> 506 us (0.979)
  waiting for transfers between devices: 161 us -> 148 us
    ppermute x35, waiting for transfers between devices: 122 us -> 109 us  [swap(): return lax.ppermute(x, axis, [(i, i ^ mask) for i in range(size)])]
    ppermute x3, waiting for transfers between devices: 22.9 us -> 11 us  [send_to_queries(): got = lax.ppermute(sent, 'pos', pairs)]
    all_gather x1, waiting for transfers between devices: 7.48 us -> 19.3 us  [body(): others = lax.all_gather(others, 'seq', axis=0, tiled=False)]
    unnamed x139 -> x143, local copies, waits for them, and re-layouts: 24.8 us -> 25.1 us
where the time goes in v2:
time: 506 us; the launch traced here: 496 us
  Pallas kernels  207 us (41%)
  waiting for transfers between devices  148 us (29%)
  starting transfers between devices  56.4 us (11%)
  local copies, waits for them, and re-layouts  37.9 us (7%)
  other arithmetic  29.2 us (6%)
  between operations  14.8 us (3%)
    ppermute x35, waiting for transfers between devices, swap(): return lax.ppermute(x, axis, [(i, i ^ mask) for i in range(size)])  109 us
    pallas_call x12, Pallas kernels, halves_sum(): pl.pallas_call(halves_kernel, grid_spec=pltpu.PrefetchScalarGridSpec(num_...  38.9 us
    pallas_call x1, Pallas kernels, feed_forward(): pl.pallas_call(functools.partial(ffn_kernel, len(parts)), grid_spec=pltpu...  37 us
    ppermute x35, starting transfers between devices, swap(): return lax.ppermute(x, axis, [(i, i ^ mask) for i in range(size)])  33.2 us
    pallas_call x3, Pallas kernels, logits_adam(): pl.pallas_call(logits_adam_kernel, grid_spec=pltpu.PrefetchScalarGridSpec...  33.1 us
    unnamed x143, local copies, waits for them, and re-layouts  25.1 us
    pallas_call x3, Pallas kernels, mix_backward(): pl.pallas_call(functools.partial(backward_kernel, blocks, split), grid_sp...  23.8 us
    pallas_call x2, Pallas kernels, weight_grads(): pl.pallas_call(functools.partial(grads_kernel, first), grid_spec=pltpu.Pr...  21.9 us
  transfers between devices with their start and end apart: 50, of which 17 were waited for; matrix products, arithmetic and copies ran while one was open for 6% of the time, Pallas kernels for 34%

profile of v2, /device:TPU:0, one launch (start us, length us, event | category | flops | bytes accessed | tf_op | source)
XLA Modules:
  0.0 496.4 jit_solution(6988310103631020095)
XLA Ops:
  16.9 8.5 %row_totals.1.refs_1_.refs_2_ = f32[16,1024]{1,0:T(8,128)} custom-call(s32[1]{0:T(128)} %bitcast.5.pos_ref, f32[12,1024,256]{2,1,0:T(8,128)} %weight_ref.5, bf16[48,384]{1,0:T(8,128)(2,1)} %bitcast.198, bf16[9,48,384]{2,1,0:T(8,128)(2,1)} %behind.40.refs_1_), custom_call_target="tpu_custom_call" | custom-call | flops 500000000 | tf_op jit(solution)/shard_map/row_totals/pallas_call | solution.py:324
  46.9 3.2 collective-permute-done.5.refs_0_
  55.6 10.7 %attention.1.refs_1_.attention_ref = bf16[12,1024,256]{2,1,0:T(8,128)(2,1)} custom-call(s32[1]{0:T(128)} %bitcast.5.pos_ref, f32[12,1024,256]{2,1,0:T(8,128)} %weight_ref.5, f32[16,1024]{1,0:T(8,128)} %add_divide_fusion.scale_ref), custom_call_target="tpu_custom_call" | custom-call | flops 500000000 | tf_op jit(solution)/shard_map/attention/pallas_call | solution.py:365
  73.2 9.0 %mix_forward.1 = (bf16[4,256,768]{2,1,0:T(8,128)(2,1)}, bf16[4,256,768]{2,1,0:T(8,128)(2,1)}, bf16[4,256,768]{2,1,0:T(8,128)(2,1)}, bf16[4,256,768]{2,1,0:T(8,128)(2,1)}) custom-call(s32[1]{0:T(128)} %bitcast.5.pos_ref, bf16[12,1024,256]{2,1,0:T(8,128)(2,1)} %attention.1.refs_1_.attention_ref, bf16[4,256,768]{2,1,0:T(8,128)(2,1)} %bitcast.192), custom_call_target="tpu_custom_call" | custom-call | flops 500000000 | tf_op jit(solution)/shard_map/mix_forward/pallas_call | solution.py:409
  84.2 3.5 collective-permute-done.8
  95.1 3.3 collective-permute-start.10
  98.4 19.3 %all-gather.6.cloned.1.call-done.refs_0_ = bf16[8,9,96,384]{3,2,1,0:T(8,128)(2,1)} async-done(((bf16[1,9,96,384]{3,2,1,0:T(8,128)(2,1)}), bf16[8,9,96,384]{3,2,1,0:T(8,128)(2,1)}) %all-gather.6.cloned.1.call-update) | async-done | bytes 5308432 | tf_op jit(solution)/shard_map/all_gather | solution.py:1027
  117.8 7.6 %collective-permute-done.11.refs_0_ = bf16[4,256,768]{2,1,0:T(8,128)(2,1)} collective-permute-done((bf16[4,256,768]{2,1,0:T(8,128)(2,1)S(1)}, bf16[4,256,768]{2,1,0:T(8,128)(2,1)}, u32[]{:S(2)}, u32[]{:S(2)}) %collective-permute-start.11) | collective-permute-done | bytes 1572896 | tf_op jit(solution)/shard_map/ppermute | solution.py:248
  126.9 37.0 %feed_forward.1 = (bf16[4,256,768]{2,1,0:T(8,128)(2,1)}, bf16[4,256,768]{2,1,0:T(8,128)(2,1)}, bf16[4,256,768]{2,1,0:T(8,128)(2,1)}, bf16[4,4,256,768]{3,2,1,0:T...) custom-call(s32[1]{0:T(128)} %bitcast.core_ref, ...), custom_call_target="tpu_custom_call" | custom-call | flops 8000000000 | tf_op jit(solution)/shard_map/feed_forward/pallas_call | solution.py:560
  166.4 9.6 %grads_down.1 = (bf16[4,768,384]{2,1,0:T(8,128)(2,1)}, bf16[4,768,384]{2,1,0:T(8,128)(2,1)}) custom-call(s32[1]{0:T(128)} %bitcast.core_ref, bf16[4,1024,768]{2,1,0:T(8,128)(2,1)} %bitcast.244, bf16[1024,768]{1,0:T(8,128)(2,1)} %bitcast.191), custom_call_target="tpu_custom_call" | custom-call | flops 8000000000 | tf_op jit(solution)/shard_map/grads_down/pallas_call | solution.py:627
  176.0 4.1 collective-permute-done.13.refs_0_
  187.6 7.9 %mix_backward.3 = (bf16[2,4,256,256]{3,2,1,0:T(8,128)(2,1)}, bf16[2,4,256,256]{3,2,1,0:T(8,128)(2,1)}, bf16[4,256,256]{2,1,0:T(8,128)(2,1)}) custom-call(s32[2]{0:T(128)} %pad_add_fusion.place_ref, bf16[12,1024,256]{2,1,0:T(8,128)(2,1)} %attention.1.refs_1_.attention_ref, bf16[4,256,768]{2,1,0:T(8,128)(2,1)} %bitcast.193, ...), custom_call_target="tpu_custom_call" | custom-call | flops 199999995904 | tf_op jit(solution)/shard_map/mix_backward/pallas_call | solution.py:722
  195.4 4.6 collective-permute-done.17.refs_0_
  206.2 7.9 %mix_backward.4 = (bf16[2,4,256,256]{3,2,1,0:T(8,128)(2,1)}, bf16[2,4,256,256]{3,2,1,0:T(8,128)(2,1)}, bf16[4,256,256]{2,1,0:T(8,128)(2,1)}) custom-call(s32[2]{0:T(128)} %pad_add_fusion.place_ref, bf16[12,1024,256]{2,1,0:T(8,128)(2,1)} %attention.1.refs_1_.attention_ref, bf16[4,256,768]{2,1,0:T(8,128)(2,1)} %bitcast.194, ...), custom_call_target="tpu_custom_call" | custom-call | flops 199999995904 | tf_op jit(solution)/shard_map/mix_backward/pallas_call | solution.py:722
  214.2 12.3 %grads_others.1 = (bf16[5,768,384]{2,1,0:T(8,128)(2,1)}, bf16[5,768,384]{2,1,0:T(8,128)(2,1)}) custom-call(s32[1]{0:T(128)} %bitcast.core_ref, bf16[1024,768]{1,0:T(8,128)(2,1)} %bitcast.247, bf16[1024,768]{1,0:T(8,128)(2,1)} %bitcast.249, bf16[1024,768]{1,0:T(8,128)(2,1)} %bitcast.248, bf16[4,1024,768]{2,1,0:T(8,128)(2,1)} %behind.52.refs_3_), custom_call_target="tpu_custom_call" | custom-call | flops 8000000000 | tf_op jit(solution)/shard_map/grads_others/pallas_call | solution.py:627
  226.5 3.7 collective-permute-done.15.refs_0_
  239.7 7.9 %mix_backward.5 = (bf16[2,4,256,256]{3,2,1,0:T(8,128)(2,1)}, bf16[2,4,256,256]{3,2,1,0:T(8,128)(2,1)}, bf16[4,256,256]{2,1,0:T(8,128)(2,1)}) custom-call(s32[2]{0:T(128)} %pad_add_fusion.place_ref, bf16[12,1024,256]{2,1,0:T(8,128)(2,1)} %attention.1.refs_1_.attention_ref, bf16[4,256,768]{2,1,0:T(8,128)(2,1)} %bitcast.195, ...), custom_call_target="tpu_custom_call" | custom-call | flops 199999995904 | tf_op jit(solution)/shard_map/mix_backward/pallas_call | solution.py:722
  249.1 7.2 %halves_sum.13 = (bf16[40,48,384]{2,1,0:T(8,128)(2,1)}, bf16[40,48,384]{2,1,0:T(8,128)(2,1)}) custom-call(s32[1]{0:T(128)} %bitcast.42.bit_ref, bf16[40,2,48,384]{3,2,1,0:T(8,128)(2,1)} %bitcast.245, bf16[40,2,48,384]{3,2,1,0:T(8,128)(2,1)} %bitcast.46.refs_1_), custom_call_target="tpu_custom_call" | custom-call | flops 8000000000 | tf_op jit(solution)/shard_map/halves_sum/pallas_call | solution.py:142
  256.8 6.7 %halves_sum.14 = (bf16[8,192,384]{2,1,0:T(8,128)(2,1)}, bf16[8,192,384]{2,1,0:T(8,128)(2,1)}) custom-call(s32[1]{0:T(128)} %bitcast.42.bit_ref, bf16[8,2,192,384]{3,2,1,0:T(8,128)(2,1)} %bitcast.246, bf16[8,2,192,384]{3,2,1,0:T(8,128)(2,1)} %bitcast.47.refs_1_), custom_call_target="tpu_custom_call" | custom-call | flops 8000000000 | tf_op jit(solution)/shard_map/halves_sum/pallas_call | solution.py:142
  270.0 8.7 %input_backward.1 = (bf16[4,256,768]{2,1,0:T(8,128)(2,1)}, f32[1,768]{1,0:T(1,128)}, bf16[1,768,384]{2,1,0:T(8,128)(2,1)}, bf16[1,768,384]{2,1,0:T(8,128)(2,1)}) custom-call(s32[1]{0:T(128)} %bitcast.core_ref, bf16[4,256,256]{2,1,0:T(8,128)(2,1)} %behind.59.refs_0_, bf16[4,256,256]{2,1,0:T(8,128)(2,1)} %get-tuple-element.114.refs_1_, ...), custom_call_target="tpu_custom_call" | custom-call | flops 8000000000 | tf_op jit(solution)/shard_map/input_backward/pallas_call | solution.py:860
  285.6 7.5 %collective-permute-done.27.refs_0_ = bf16[1024,256]{1,0:T(8,128)(2,1)} collective-permute-done((bf16[1024,256]{1,0:T(8,128)(2,1)}, bf16[1024,256]{1,0:T(8,128)(2,1)}, u32[]{:S(2)}, u32[]{:S(2)}) %collective-permute-start.27) | collective-permute-done | bytes 524320 | tf_op jit(solution)/shard_map/ppermute | solution.py:45
  306.0 3.2 halves_sum.20
  309.8 22.1 %collective-permute-done.32.refs_0_ = bf16[1024,256]{1,0:T(8,128)(2,1)S(1)} collective-permute-done((bf16[1024,256]{1,0:T(8,128)(2,1)}, bf16[1024,256]{1,0:T(8,128)(2,1)S(1)}, u32[]{:S(2)}, u32[]{:S(2)}) %collective-permute-start.32) | collective-permute-done | bytes 524320 | tf_op jit(solution)/shard_map/ppermute | solution.py:45
  335.8 6.0 %merge_halves.1 = (bf16[4,5,48,384]{3,2,1,0:T(8,128)(2,1)}, bf16[4,5,48,384]{3,2,1,0:T(8,128)(2,1)}) custom-call(s32[1]{0:T(128)} %bitcast.28.bit_ref, bf16[4,2,4,48,384]{4,3,2,1,0:T(8,128)(2,1)} %bitcast.252, bf16[4,2,4,48,384]{4,3,2,1,0:T(8,128)(2,1)} %bitcast.71.got, bf16[4,2,1,48,384]{4,3,2,1,0:T(8,128)(2,1)} %bitcast.263, ...), custom_call_target="tpu_custom_call" | custom-call | flops 8000000000 | tf_op jit(solution)/shard_map/merge_halves/pallas_call | solution.py:932
  344.2 3.1 collective-permute-done.35
  347.9 6.5 %collective-permute-done.39.refs_3_ = bf16[512,256]{1,0:T(8,128)(2,1)S(1)} collective-permute-done((bf16[512,256]{1,0:T(8,128)(2,1)}, bf16[512,256]{1,0:T(8,128)(2,1)S(1)}, u32[]{:S(2)}, u32[]{:S(2)}) %collective-permute-start.39) | collective-permute-done | bytes 262176 | tf_op jit(solution)/shard_map/ppermute | solution.py:45
  357.3 11.2 %logits_adam.3 = (f32[12,1024,256]{2,1,0:T(8,128)}, f32[12,1024,256]{2,1,0:T(8,128)}, f32[12,1024,256]{2,1,0:T(8,128)}) custom-call(s32[2]{0:T(128)} %pad_add_fusion.place_ref, f32[12,1024,256]{2,1,0:T(8,128)} %weight_ref.5, f32[12,1024,256]{2,1,0:T(8,128)} %first_ref.5, f32[12,1024,256]{2,1,0:T(8,128)} %second_ref.5, ...), custom_call_target="tpu_custom_call" | custom-call | flops 20000000000 | tf_op jit(solution)/shard_map/logits_adam/pallas_call | solution.py:807
  370.2 4.0 bundle.1
  383.5 17.5 %collective-permute-done.40 = f32[2,768]{1,0:T(2,128)S(1)} collective-permute-done((f32[2,768]{1,0:T(2,128)}, f32[2,768]{1,0:T(2,128)S(1)}, u32[]{:S(2)}, u32[]{:S(2)}) %collective-permute-start.40) | collective-permute-done | bytes 6176 | tf_op jit(solution)/shard_map/ppermute | solution.py:45
  407.8 38.6 %collective-permute-done.42 = f32[2,768]{1,0:T(2,128)S(1)} collective-permute-done((f32[2,768]{1,0:T(2,128)}, f32[2,768]{1,0:T(2,128)S(1)}, u32[]{:S(2)}, u32[]{:S(2)}) %collective-permute-start.42) | collective-permute-done | bytes 6176 | tf_op jit(solution)/shard_map/ppermute | solution.py:45
  455.6 10.9 %logits_adam.4 = (f32[12,1024,256]{2,1,0:T(8,128)}, f32[12,1024,256]{2,1,0:T(8,128)}, f32[12,1024,256]{2,1,0:T(8,128)}) custom-call(s32[2]{0:T(128)} %pad_add_fusion.place_ref, f32[12,1024,256]{2,1,0:T(8,128)} %weight_ref.5, f32[12,1024,256]{2,1,0:T(8,128)} %first_ref.5, ...), custom_call_target="tpu_custom_call", output_to_operand_aliasing={{0}: (8, {}), {1}: (9, {}), {2}: (10, {})} | custom-call | flops 20000000000 | tf_op jit(solution)/shard_map/logits_adam/pallas_call | solution.py:807
  468.7 11.0 %logits_adam.5 = (f32[12,1024,256]{2,1,0:T(8,128)}, f32[12,1024,256]{2,1,0:T(8,128)}, f32[12,1024,256]{2,1,0:T(8,128)}) custom-call(s32[2]{0:T(128)} %pad_add_fusion.place_ref, f32[12,1024,256]{2,1,0:T(8,128)} %weight_ref.5, f32[12,1024,256]{2,1,0:T(8,128)} %first_ref.5, ...), custom_call_target="tpu_custom_call", output_to_operand_aliasing={{0}: (8, {}), {1}: (9, {}), {2}: (10, {})} | custom-call | flops 20000000000 | tf_op jit(solution)/shard_map/logits_adam/pallas_call | solution.py:807
  (338 shorter events, 157.1 us)
Async XLA Ops:
  7.2 110.6 %all-gather.6.cloned.1.call-start = ((), (), s32[]{:S(2)}) async-start(), calls=%async_computation | async-start | bytes 5971968 | tf_op jit(solution)/shard_map/all_gather | solution.py:1027
  28.7 328.5 %all-gather.8.cloned.1.call-start = ((), (), s32[]{:S(2)}) async-start(), calls=%async_computation.1 | async-start | bytes 2359296 | tf_op jit(solution)/shard_map/all_gather | solution.py:1217
  39.3 14.2 %collective-permute-start.3 = (f32[16,1024]{1,0:T(8,128)S(1)}, f32[16,1024]{1,0:T(8,128)S(1)}, u32[]{:S(2)}, u32[]{:S(2)}) collective-permute-start(f32[16,1024]{1,0:T(8,128)S(1)} %add.126.refs_1_), channel_id=1, source_target_pairs={{0,16},{8,24},{16,0},{24,8},{1,17},{9,25},{17,1},{25,9},{2,18},{10... | collective-permute-start | bytes 196616 | tf_op jit(solution)/shard_map/ppermute | solution.py:45
  51.8 14.5 %collective-permute-start.6 = (bf16[2,2,2,48,384]{4,3,2,1,0:T(8,128)(2,1)S(1)}, bf16[2,2,2,48,384]{4,3,2,1,0:T(8,128)(2,1)S(1)}, u32[]{:S(2)}, u32[]{:S(2)}) collective-permute-start(bf16[2,2,2,48,384]{4,3,2,1,0:T(8,128)(2,1)S(1)} %maximum_select_fusion.5.refs_1_), channel_id=1, source_target_pairs={{0,1},{1,0},{2,3},{3,2},{4,5},{5,4},{6,7},{7,6},{8,9},{9,8},{10,11... | collective-permute-start | bytes 884744 | tf_op jit(solution)/shard_map/ppermute | solution.py:45
  89.6 35.8 %collective-permute-start.11 = (bf16[4,256,768]{2,1,0:T(8,128)(2,1)S(1)}, bf16[4,256,768]{2,1,0:T(8,128)(2,1)}, u32[]{:S(2)}, u32[]{:S(2)}) collective-permute-start(bf16[4,256,768]{2,1,0:T(8,128)(2,1)S(1)} %add_convert_fusion.refs_1_), channel_id=1, source_target_pairs={{0,16},{8,24},{1,17},{9,25},{2,18},{10,26},{3,19},{11,27},{4,20},{... | collective-permute-start | bytes 4718600 | tf_op jit(solution)/shard_map/ppermute | solution.py:248
  95.1 30.3 %collective-permute-start.10 = (bf16[4,256,768]{2,1,0:T(8,128)(2,1)}, bf16[4,256,768]{2,1,0:T(8,128)(2,1)}, u32[]{:S(2)}, u32[]{:S(2)}) collective-permute-start(bf16[4,256,768]{2,1,0:T(8,128)(2,1)} %get-tuple-element.90), channel_id=1, source_target_pairs={{0,8},{16,24},{1,9},{17,25},{2,10},{18,26},{3,11},{19,27},{4,12},{... | collective-permute-start | bytes 4718600 | tf_op jit(solution)/shard_map/ppermute | solution.py:248
  163.8 16.2 %collective-permute-start.13 = (bf16[1,1040,256]{2,1,0:T(8,128)(2,1)}, bf16[1,1040,256]{2,1,0:T(8,128)(2,1)S(1)}, u32[]{:S(2)}, u32[]{:S(2)}) collective-permute-start(bf16[1,1040,256]{2,1,0:T(8,128)(2,1)} %get-tuple-element.92.refs_0_.refs_4_), channel_id=1, source_target_pairs={{16,0},{24,8},{17,1},{25,9},{18,2},{26,10},{19,3},{27,11},{20,4},{... | collective-permute-start | bytes 1597448 | tf_op jit(solution)/shard_map/ppermute | solution.py:267
  165.1 20.8 %collective-permute-start.12 = (bf16[1,1040,256]{2,1,0:T(8,128)(2,1)}, bf16[1,1040,256]{2,1,0:T(8,128)(2,1)S(1)}, u32[]{:S(2)}, u32[]{:S(2)}) collective-permute-start(bf16[1,1040,256]{2,1,0:T(8,128)(2,1)} %get-tuple-element.92.refs_0_.refs_4_), channel_id=1, source_target_pairs={{8,0},{24,16},{9,1},{25,17},{10,2},{26,18},{11,3},{27,19},{12,4},{... | collective-permute-start | bytes 1597448 | tf_op jit(solution)/shard_map/ppermute | solution.py:267
  183.4 16.7 %collective-permute-start.17 = (bf16[1,1040,256]{2,1,0:T(8,128)(2,1)}, bf16[1,1040,256]{2,1,0:T(8,128)(2,1)}, u32[]{:S(2)}, u32[]{:S(2)}) collective-permute-start(bf16[1,1040,256]{2,1,0:T(8,128)(2,1)} %get-tuple-element.102.refs_0_.refs_4_), channel_id=1, source_target_pairs={{16,0},{24,8},{17,1},{25,9},{18,2},{26,10},{19,3},{27,11},{20,4},{... | collective-permute-start | bytes 1597448 | tf_op jit(solution)/shard_map/ppermute | solution.py:267
  184.7 20.8 %collective-permute-start.16 = (bf16[1,1040,256]{2,1,0:T(8,128)(2,1)}, bf16[1,1040,256]{2,1,0:T(8,128)(2,1)}, u32[]{:S(2)}, u32[]{:S(2)}) collective-permute-start(bf16[1,1040,256]{2,1,0:T(8,128)(2,1)} %get-tuple-element.102.refs_0_.refs_4_), channel_id=1, source_target_pairs={{8,0},{24,16},{9,1},{25,17},{10,2},{26,18},{11,3},{27,19},{12,4},{... | collective-permute-start | bytes 1597448 | tf_op jit(solution)/shard_map/ppermute | solution.py:267
  202.0 31.0 %collective-permute-start.23 = (bf16[1,1040,256]{2,1,0:T(8,128)(2,1)}, bf16[1,1040,256]{2,1,0:T(8,128)(2,1)}, u32[]{:S(2)}, u32[]{:S(2)}) collective-permute-start(bf16[1,1040,256]{2,1,0:T(8,128)(2,1)} %get-tuple-element.109.refs_0_.refs_4_), channel_id=1, source_target_pairs={{16,0},{24,8},{17,1},{25,9},{18,2},{26,10},{19,3},{27,11},{20,4},{... | collective-permute-start | bytes 1597448 | tf_op jit(solution)/shard_map/ppermute | solution.py:267
  203.3 35.3 %collective-permute-start.22 = (bf16[1,1040,256]{2,1,0:T(8,128)(2,1)}, bf16[1,1040,256]{2,1,0:T(8,128)(2,1)}, u32[]{:S(2)}, u32[]{:S(2)}) collective-permute-start(bf16[1,1040,256]{2,1,0:T(8,128)(2,1)} %get-tuple-element.109.refs_0_.refs_4_), channel_id=1, source_target_pairs={{8,0},{24,16},{9,1},{25,17},{10,2},{26,18},{11,3},{27,19},{12,4},{... | collective-permute-start | bytes 1597448 | tf_op jit(solution)/shard_map/ppermute | solution.py:267
  204.8 25.4 %collective-permute-start.15 = (bf16[2048,256]{1,0:T(8,128)(2,1)}, bf16[2048,256]{1,0:T(8,128)(2,1)}, u32[]{:S(2)}, u32[]{:S(2)}) collective-permute-start(bf16[2048,256]{1,0:T(8,128)(2,1)} %bitcast.34), channel_id=1, source_target_pairs={{0,1},{1,0},{2,3},{3,2},{4,5},{5,4},{6,7},{7,6},{8,9},{9,8},{10,11... | collective-permute-start | bytes 3145736 | tf_op jit(solution)/shard_map/ppermute | solution.py:45
  237.5 19.3 %collective-permute-start.20 = (bf16[4,768,384]{2,1,0:T(8,128)(2,1)}, bf16[4,768,384]{2,1,0:T(8,128)(2,1)}, u32[]{:S(2)}, u32[]{:S(2)}) collective-permute-start(bf16[4,768,384]{2,1,0:T(8,128)(2,1)} %get-tuple-element.108), channel_id=1, source_target_pairs={{0,8},{8,0},{16,24},{24,16},{1,9},{9,1},{17,25},{25,17},{2,10},{10... | collective-permute-start | bytes 7077896 | tf_op jit(solution)/shard_map/ppermute | solution.py:45
  238.0 40.7 %collective-permute-start.26 = (bf16[2048,256]{1,0:T(8,128)(2,1)}, bf16[2048,256]{1,0:T(8,128)(2,1)}, u32[]{:S(2)}, u32[]{:S(2)}) collective-permute-start(bf16[2048,256]{1,0:T(8,128)(2,1)} %bitcast.53), channel_id=1, source_target_pairs={{0,1},{1,0},{2,3},{3,2},{4,5},{5,4},{6,7},{7,6},{8,9},{9,8},{10,11... | collective-permute-start | bytes 3145736 | tf_op jit(solution)/shard_map/ppermute | solution.py:45
  238.5 26.6 %collective-permute-start.19 = (bf16[1024,256]{1,0:T(8,128)(2,1)}, bf16[1024,256]{1,0:T(8,128)(2,1)}, u32[]{:S(2)}, u32[]{:S(2)}) collective-permute-start(bf16[1024,256]{1,0:T(8,128)(2,1)} %bitcast.41.refs_1_), channel_id=1, source_target_pairs={{0,2},{1,3},{2,0},{3,1},{4,6},{5,7},{6,4},{7,5},{8,10},{9,11},{10,... | collective-permute-start | bytes 1572872 | tf_op jit(solution)/shard_map/ppermute | solution.py:45
  247.6 51.9 %collective-permute-start.31 = (bf16[2048,256]{1,0:T(8,128)(2,1)}, bf16[2048,256]{1,0:T(8,128)(2,1)S(1)}, u32[]{:S(2)}, u32[]{:S(2)}) collective-permute-start(bf16[2048,256]{1,0:T(8,128)(2,1)} %bitcast.225), channel_id=1, source_target_pairs={{0,1},{1,0},{2,3},{3,2},{4,5},{5,4},{6,7},{7,6},{8,9},{9,8},{10,11... | collective-permute-start | bytes 3145736 | tf_op jit(solution)/shard_map/ppermute | solution.py:45
  256.4 48.5 %collective-permute-start.33 = (bf16[40,48,384]{2,1,0:T(8,128)(2,1)}, bf16[40,48,384]{2,1,0:T(8,128)(2,1)S(1)}, u32[]{:S(2)}, u32[]{:S(2)}) collective-permute-start(bf16[40,48,384]{2,1,0:T(8,128)(2,1)} %get-tuple-element.111.refs_1_), channel_id=1, source_target_pairs={{0,16},{8,24},{16,0},{24,8},{1,17},{9,25},{17,1},{25,9},{2,18},{10... | collective-permute-start | bytes 4423688 | tf_op jit(solution)/shard_map/ppermute | solution.py:45
  263.5 71.6 %collective-permute-start.30 = (bf16[8,192,384]{2,1,0:T(8,128)(2,1)}, bf16[8,192,384]{2,1,0:T(8,128)(2,1)}, u32[]{:S(2)}, u32[]{:S(2)}) collective-permute-start(bf16[8,192,384]{2,1,0:T(8,128)(2,1)} %get-tuple-element.112.refs_1_), channel_id=1, source_target_pairs={{0,16},{8,24},{16,0},{24,8},{1,17},{9,25},{17,1},{25,9},{2,18},{10... | collective-permute-start | bytes 3538952 | tf_op jit(solution)/shard_map/ppermute | solution.py:45
  267.2 15.4 %collective-permute-start.28 = (bf16[512,256]{1,0:T(8,128)(2,1)}, bf16[512,256]{1,0:T(8,128)(2,1)S(1)}, u32[]{:S(2)}, u32[]{:S(2)}) collective-permute-start(bf16[512,256]{1,0:T(8,128)(2,1)} %bitcast.241), channel_id=1, source_target_pairs={{0,4},{1,5},{2,6},{3,7},{4,0},{5,1},{6,2},{7,3},{8,12},{9,13},{10,... | collective-permute-start | bytes 786440 | tf_op jit(solution)/shard_map/ppermute | solution.py:45
  285.1 170.5 %all-gather.10.cloned.1.call-start = ((), (), s32[]{:S(2)}) async-start(), calls=%async_computation.2 | async-start | bytes 4718592 | tf_op jit(solution)/shard_map/all_gather | solution.py:1217
  295.2 48.3 %collective-permute-start.38 = (bf16[512,256]{1,0:T(8,128)(2,1)}, bf16[512,256]{1,0:T(8,128)(2,1)S(1)}, u32[]{:S(2)}, u32[]{:S(2)}) collective-permute-start(bf16[512,256]{1,0:T(8,128)(2,1)} %bitcast.237), channel_id=1, source_target_pairs={{0,4},{1,5},{2,6},{3,7},{4,0},{5,1},{6,2},{7,3},{8,12},{9,13},{10,... | collective-permute-start | bytes 786440 | tf_op jit(solution)/shard_map/ppermute | solution.py:45
  297.9 37.2 %collective-permute-start.34 = (bf16[8,48,384]{2,1,0:T(8,128)(2,1)}, bf16[8,48,384]{2,1,0:T(8,128)(2,1)S(1)}, u32[]{:S(2)}, u32[]{:S(2)}) collective-permute-start(bf16[8,48,384]{2,1,0:T(8,128)(2,1)} %get-tuple-element.127.refs_1_), channel_id=1, source_target_pairs={{0,16},{8,24},{16,0},{24,8},{1,17},{9,25},{17,1},{25,9},{2,18},{10... | collective-permute-start | bytes 884744 | tf_op jit(solution)/shard_map/ppermute | solution.py:45
  303.3 28.7 %collective-permute-start.32 = (bf16[1024,256]{1,0:T(8,128)(2,1)}, bf16[1024,256]{1,0:T(8,128)(2,1)S(1)}, u32[]{:S(2)}, u32[]{:S(2)}) collective-permute-start(bf16[1024,256]{1,0:T(8,128)(2,1)} %bitcast.232), channel_id=1, source_target_pairs={{0,2},{1,3},{2,0},{3,1},{4,6},{5,7},{6,4},{7,5},{8,10},{9,11},{10,... | collective-permute-start | bytes 1572872 | tf_op jit(solution)/shard_map/ppermute | solution.py:45
  309.2 60.1 %collective-permute-start.36 = (bf16[20,48,384]{2,1,0:T(8,128)(2,1)}, bf16[20,48,384]{2,1,0:T(8,128)(2,1)S(1)}, u32[]{:S(2)}, u32[]{:S(2)}) collective-permute-start(bf16[20,48,384]{2,1,0:T(8,128)(2,1)} %get-tuple-element.133.refs_1_), channel_id=1, source_target_pairs={{0,1},{1,0},{2,3},{3,2},{4,5},{5,4},{6,7},{7,6},{8,9},{9,8},{10,11... | collective-permute-start | bytes 2211848 | tf_op jit(solution)/shard_map/ppermute | solution.py:45
  334.9 19.6 %collective-permute-start.39 = (bf16[512,256]{1,0:T(8,128)(2,1)}, bf16[512,256]{1,0:T(8,128)(2,1)S(1)}, u32[]{:S(2)}, u32[]{:S(2)}) collective-permute-start(bf16[512,256]{1,0:T(8,128)(2,1)} %bitcast.239), channel_id=1, source_target_pairs={{0,4},{1,5},{2,6},{3,7},{4,0},{5,1},{6,2},{7,3},{8,12},{9,13},{10,... | collective-permute-start | bytes 786440 | tf_op jit(solution)/shard_map/ppermute | solution.py:45
  341.8 26.6 %collective-permute-start.37 = (bf16[4,5,48,384]{3,2,1,0:T(8,128)(2,1)}, bf16[4,5,48,384]{3,2,1,0:T(8,128)(2,1)S(1)}, u32[]{:S(2)}, u32[]{:S(2)}) collective-permute-start(bf16[4,5,48,384]{3,2,1,0:T(8,128)(2,1)} %get-tuple-element.136.refs_1_), channel_id=1, source_target_pairs={{0,1},{1,0},{2,3},{3,2},{4,5},{5,4},{6,7},{7,6},{8,9},{9,8},{10,11... | collective-permute-start | bytes 2211848 | tf_op jit(solution)/shard_map/ppermute | solution.py:45
  376.8 24.9 %collective-permute-start.41 = (bf16[2,480,384]{2,1,0:T(8,128)(2,1)}, bf16[2,480,384]{2,1,0:T(8,128)(2,1)S(1)}, u32[]{:S(2)}, u32[]{:S(2)}) collective-permute-start(bf16[2,480,384]{2,1,0:T(8,128)(2,1)} %get-tuple-element.142.refs_1_), channel_id=1, source_target_pairs={{0,2},{1,3},{2,0},{3,1},{4,6},{5,7},{6,4},{7,5},{8,10},{9,11},{10,... | collective-permute-start | bytes 2211848 | tf_op jit(solution)/shard_map/ppermute | solution.py:45
  377.1 23.9 %collective-permute-start.40 = (f32[2,768]{1,0:T(2,128)}, f32[2,768]{1,0:T(2,128)S(1)}, u32[]{:S(2)}, u32[]{:S(2)}) collective-permute-start(f32[2,768]{1,0:T(2,128)} %behind.73.refs_1_), channel_id=1, source_target_pairs={{0,2},{1,3},{2,0},{3,1},{4,6},{5,7},{6,4},{7,5},{8,10},{9,11},{10,... | collective-permute-start | bytes 18440 | tf_op jit(solution)/shard_map/ppermute | solution.py:45
  404.9 42.8 %collective-permute-start.43 = (bf16[1,480,384]{2,1,0:T(8,128)(2,1)}, bf16[1,480,384]{2,1,0:T(8,128)(2,1)S(1)}, u32[]{:S(2)}, u32[]{:S(2)}) collective-permute-start(bf16[1,480,384]{2,1,0:T(8,128)(2,1)} %get-tuple-element.144.refs_1_), channel_id=1, source_target_pairs={{0,4},{1,5},{2,6},{3,7},{4,0},{5,1},{6,2},{7,3},{8,12},{9,13},{10,... | collective-permute-start | bytes 1105928 | tf_op jit(solution)/shard_map/ppermute | solution.py:45
  407.3 39.1 %collective-permute-start.42 = (f32[2,768]{1,0:T(2,128)}, f32[2,768]{1,0:T(2,128)S(1)}, u32[]{:S(2)}, u32[]{:S(2)}) collective-permute-start(f32[2,768]{1,0:T(2,128)} %behind.75.refs_1_), channel_id=1, source_target_pairs={{0,4},{1,5},{2,6},{3,7},{4,0},{5,1},{6,2},{7,3},{8,12},{9,13},{10,... | collective-permute-start | bytes 18440 | tf_op jit(solution)/shard_map/ppermute | solution.py:45
  451.9 14.5 %collective-permute-start.45 = (bf16[10,48,384]{2,1,0:T(8,128)(2,1)S(1)}, bf16[10,48,384]{2,1,0:T(8,128)(2,1)S(1)}, u32[]{:S(2)}, u32[]{:S(2)}) collective-permute-start(bf16[10,48,384]{2,1,0:T(8,128)(2,1)S(1)} %bitcast.210), channel_id=1, source_target_pairs={{0,16},{8,24},{16,0},{24,8},{1,17},{9,25},{17,1},{25,9},{2,18},{10... | collective-permute-start | bytes 1105928 | tf_op jit(solution)/shard_map/ppermute | solution.py:45
  (86 other events, 296.1 us)
Sparse Core Ops, SparseCore 0:
  28.9 88.8 all-gather.5
  285.2 68.6 all-gather.7
  357.4 97.4 all-gather.9
